TPU v7x, 256 devices: a whole 4x4x8 slice. The times are simulated.
256 devices in a mesh: rep: 32 (over y_lo, z, core), fsdp: 8 (over y_hi, x).
Axes of the slice: x: 4, y: 4 (y_hi: 2, y_lo: 2; y = y_hi * 2 + y_lo), z: 8, core: 2. Of those that a mesh axis runs over, the one named last changes fastest.
Arguments:
- tokens: bfloat16 [65536, 5120], P(('rep', 'fsdp')), may hold values from -6 to 6
- value_cotangent: bfloat16 [65536, 512], P(('rep', 'fsdp')), may hold values from -6 to 6
- value_weight: bfloat16 [32, 5120, 512], P('rep', 'fsdp'), may hold values from -0.078125 to 0.078125
- outer_delta: float32 [32, 5120, 512], P('rep', 'fsdp'), may hold values from -3 to 3
- momentum: float32 [5120, 512], P('fsdp'), may hold values from -3 to 3
- global_weight: float32 [5120, 512], P('fsdp'), may hold values from -3 to 3
Outputs:
- values: bfloat16 [65536, 512], P(('rep', 'fsdp'))
- token_grad: bfloat16 [65536, 5120], P(('rep', 'fsdp'))
- weight_grad: bfloat16 [32, 5120, 512], P('rep', 'fsdp')
- new_momentum: float32 [5120, 512], P('fsdp')
- new_global: float32 [5120, 512], P('fsdp')
All inputs are finite; a program needn't handle non-finite values.
Results may differ from a plain program's by a relative error of at most 0.007.
Values may be sent and summed in bfloat16 or wider, within the bound.
No kernel may reach another device: no remote copies, remote signals or barrier semaphores. Data moves between devices by JAX's collectives and lax.ppermute only.
A program may use at most 128 MiB of HBM per device.

v0:
```python
import jax
import jax.numpy as jnp
from jax import lax
from jax.sharding import PartitionSpec as P


def local(tokens, value_cotangent, value_weight, outer_delta, momentum, global_weight):
    full_weight = lax.all_gather(value_weight[0], "fsdp", axis=0, tiled=True)
    values = jnp.dot(tokens, full_weight, preferred_element_type=jnp.float32).astype(jnp.bfloat16)
    token_grad = lax.dot_general(
        value_cotangent, full_weight, (((1,), (1,)), ((), ())), preferred_element_type=jnp.float32
    ).astype(jnp.bfloat16)
    weight_sum = lax.psum_scatter(
        lax.dot_general(
            tokens, value_cotangent, (((0,), (0,)), ((), ())), preferred_element_type=jnp.float32
        ),
        "fsdp",
        scatter_dimension=0,
        tiled=True,
    )
    weight_grad = weight_sum.astype(jnp.bfloat16)[None]
    replicas = lax.axis_size("rep")
    total = lax.psum(outer_delta[0].astype(jnp.bfloat16), "rep").astype(jnp.float32)
    average = total / jnp.float32(replicas)
    new_momentum = 0.9 * momentum + average
    new_global = global_weight - 0.7 * (average + 0.9 * new_momentum)
    return (values, token_grad, weight_grad, new_momentum, new_global)


def solution(mesh):
    in_specs = (
        P(("rep", "fsdp"), None),
        P(("rep", "fsdp"), None),
        P("rep", "fsdp", None),
        P("rep", "fsdp", None),
        P("fsdp", None),
        P("fsdp", None),
    )
    out_specs = (
        P(("rep", "fsdp"), None),
        P(("rep", "fsdp"), None),
        P("rep", "fsdp", None),
        P("fsdp", None),
        P("fsdp", None),
    )
    return jax.shard_map(local, mesh=mesh, in_specs=in_specs, out_specs=out_specs, check_vma=False)
```

profile of v0, /device:TPU:1, one launch (start us, length us, event | category | flops | bytes accessed | tf_op | source)
XLA Modules:
  0.0 257.5 jit_solution(14417117358597419043)
XLA Ops:
  8.0 0.0 copy-start
  8.0 0.0 copy-start.2
  8.0 0.0 all-reduce.2.cloned.1.call-start
  8.1 2.4 convert_bitcast_fusion
  10.5 0.0 all-reduce.2.cloned.1.call-update
  10.5 0.0 all-gather.3.cloned.1.call-start
  10.5 0.5 all-gather.3.cloned.1.call-update
  11.1 0.0 reduce-scatter.2.cloned.1.call-start
  11.1 0.0 copy-done
  11.1 0.0 copy-done.2
  11.1 5.5 %fusion.8 = f32[5120,512]{1,0:T(8,128)} fusion(bf16[256,5120]{1,0:T(8,128)(2,1)S(1)} %copy-done, bf16[256,512]{1,0:T(8,128)(2,1)S(1)} %copy-done.2), kind=kOutput, calls=%fused_computation.10 | convolution fusion | flops 1342177280 | bytes 13369344 | tf_op jit(solution)/shard_map/dot_general | solution.py:14
  16.7 0.0 reduce-scatter.2.cloned.1.call-update
  16.7 219.3 %all-reduce.2.cloned.1.call-done = bf16[640,512]{1,0:T(8,128)(2,1)} async-done(((bf16[640,512]{1,0:T(8,128)(2,1)}), bf16[640,512]{1,0:T(8,128)(2,1)}) %all-reduce.2.cloned.1.call-update) | async-done | bytes 655376 | tf_op jit(solution)/shard_map/psum | solution.py:23
  235.9 3.9 %multiply_subtract_fusion = (f32[640,512]{1,0:T(8,128)}, f32[640,512]{1,0:T(8,128)}) fusion(f32[640,512]{1,0:T(8,128)} %param.11, bf16[640,512]{1,0:T(8,128)(2,1)} %all-reduce.2.cloned.1.call-done, f32[640,512]{1,0:T(8,128)} %param.10), kind=kLoop, calls=%fused_computation.4 | loop fusion | flops 2621440 | bytes 5898240 | tf_op jit(solution)/shard_map/sub | solution.py:26
  239.9 0.0 all-gather.3.cloned.1.call-done
  239.9 0.0 copy-start.1
  239.9 5.7 %convolution_convert_fusion = bf16[256,5120]{1,0:T(8,128)(2,1)} fusion(bf16[256,512]{1,0:T(8,128)(2,1)S(1)} %copy-done.2, bf16[1,5120,512]{2,1,0:T(8,128)(2,1)} %all-gather.3.cloned.1.call-done), kind=kOutput, calls=%fused_computation | convolution fusion | flops 1343488000 | bytes 8126464 | tf_op jit(solution)/shard_map/dot_general | solution.py:10
  245.6 0.0 copy-done.1
  245.6 2.2 fusion.4
  247.8 0.0 reduce-scatter.2.cloned.1.call-done
  247.8 2.2 convert_bitcast_fusion.1
Async XLA Ops:
  8.0 3.1 %copy-start = (bf16[256,5120]{1,0:T(8,128)(2,1)S(1)}, bf16[256,5120]{1,0:T(8,128)(2,1)}, u32[]{:S(2)}) copy-start(bf16[256,5120]{1,0:T(8,128)(2,1)} %param.6) | copy-start | bytes 7864324
  8.0 3.1 %copy-start.2 = (bf16[256,512]{1,0:T(8,128)(2,1)S(1)}, bf16[256,512]{1,0:T(8,128)(2,1)}, u32[]{:S(2)}) copy-start(bf16[256,512]{1,0:T(8,128)(2,1)} %param.7) | copy-start | bytes 786436
  8.0 227.9 %all-reduce.2.cloned.1.call-start = ((), (), s32[]{:S(2)}) async-start(), calls=%async_computation.2 | async-start | bytes 1310720 | tf_op jit(solution)/shard_map/psum | solution.py:23
  10.5 229.4 %all-gather.3.cloned.1.call-start = ((), (), s32[]{:S(2)}) async-start(), calls=%async_computation.3 | async-start | bytes 5898240 | tf_op jit(solution)/shard_map/all_gather | solution.py:8
  11.1 236.8 %reduce-scatter.2.cloned.1.call-start = ((), (), s32[]{:S(2)}) async-start(), calls=%async_computation.1 | async-start | bytes 11796480 | tf_op jit(solution)/shard_map/reduce_scatter | solution.py:13
  239.9 5.7 %copy-start.1 = (bf16[1,5120,512]{2,1,0:T(8,128)(2,1)S(1)}, bf16[1,5120,512]{2,1,0:T(8,128)(2,1)}, u32[]{:S(2)}) copy-start(bf16[1,5120,512]{2,1,0:T(8,128)(2,1)} %all-gather.3.cloned.1.call-done) | copy-start | bytes 15728644
Sparse Core Ops, SparseCore 0:
  12.2 223.6 all-reduce.1
Sparse Core Ops, SparseCore 1:
  13.6 89.8 all-gather.2
  107.4 134.5 reduce-scatter.1
where the time goes:
time: 258 us; the launch traced here: 257 us
  waiting for transfers between devices  220 us (85%)
  between operations  15.5 us (6%)
  matrix products  13.5 us (5%)
  other arithmetic  8.53 us (3%)
    psum x1, waiting for transfers between devices, local(): lax.psum(outer_delta[0].astype(jnp.bfloat16), 'rep').astype(jnp.float32)  219 us
    dot_general x1, matrix products, local(): lax.dot_general(value_cotangent, full_weight, (((1,), (1,)), ((), ())), p...  5.74 us
    dot_general x1, matrix products, local(): lax.dot_general(tokens, value_cotangent, (((0,), (0,)), ((), ())), prefer...  5.53 us
  transfers between devices with their start and end apart: 3, of which 1 were waited for; matrix products, arithmetic and copies ran while one was open for 7% of the time, Pallas kernels for 0%

commit v1 on v0

v1 whole, which is shorter than its diff:
```python
import itertools

import jax
import jax.numpy as jnp
from jax import lax
from jax.experimental import pallas as pl
from jax.experimental.pallas import tpu as pltpu
from jax.sharding import PartitionSpec as P

AXES = ("rep", "fsdp")
GRID = (2, 8, 2, 2, 4)
F32, BF16 = jnp.float32, jnp.bfloat16


def flat(place):
    index = 0
    for coordinate, size in zip(place, GRID):
        index = index * size + coordinate % size
    return index


def permutation(move):
    return [(flat(c), flat(move(*c))) for c in itertools.product(*map(range, GRID))]


def along_x(step):
    return permutation(lambda l, z, c, h, x: (l, z, c, h, x + step))


def along_z(step):
    return permutation(lambda l, z, c, h, x: (l, z + step, c, h, x))


def flip(dl, dz, dc, dh):
    return permutation(lambda l, z, c, h, x: (l ^ dl, z ^ dz, c ^ dc, h ^ dh, x))


def send(value, moves):
    return lax.ppermute(value, AXES, moves)


def dot_t(a, b):
    return lax.dot_general(a, b, (((0,), (0,)), ((), ())), preferred_element_type=F32)


def whole(shape):
    return pl.BlockSpec(shape, lambda i, s: (0,) * len(shape))


def call(kernel, scalars, operands, specs, outs, out_specs, flops, moved, aliases={}):
    return pl.pallas_call(
        kernel,
        grid_spec=pltpu.PrefetchScalarGridSpec(
            num_scalar_prefetch=1, grid=(1,), in_specs=specs, out_specs=out_specs
        ),
        out_shape=outs,
        input_output_aliases=aliases,
        cost_estimate=pl.CostEstimate(flops=flops, bytes_accessed=moved, transcendentals=0),
        compiler_params=pltpu.CompilerParams(vmem_limit_bytes=40 * 2**20),
    )(scalars, *operands)


def local(tokens, value_cotangent, value_weight, outer_delta, momentum, global_weight):
    rep, fsdp = lax.axis_index("rep"), lax.axis_index("fsdp")
    y_lo, z, core = rep // 16, (rep // 2) % 8, rep % 2
    y_hi, x = fsdp // 4, fsdp % 4
    rows, feats = value_weight.shape[1:]
    toks = tokens.shape[0]
    half = rows // 2
    weight = value_weight[0]

    def ring(own):
        left = send(own, along_x(1))
        right = send(own, along_x(-1))
        return left, right

    def ring_on(left, right):
        top = send(left[:half], along_x(1))
        bottom = send(right[half:], along_x(-1))
        return top, bottom

    def column(plane, r):
        return plane * 4 + (x + r) % 4

    def block_for_partner(r):
        return lax.dynamic_slice(
            tokens, (0, column(1 - y_hi, r) * rows), (toks, rows)
        )

    across = flip(0, 0, 0, 1)
    left0, right0 = ring(weight)
    got = send(jnp.concatenate([value_cotangent, block_for_partner(2)], axis=1), across)
    g_other, x_other2 = got[:, :feats], got[:, feats:]
    weight1 = send(weight, across)
    got = send(
        jnp.concatenate([block_for_partner(1), block_for_partner(3), block_for_partner(0)], axis=1),
        across,
    )
    x_other130 = got

    top0, bottom0 = ring_on(left0, right0)

    scal_w = jnp.stack([column(y_hi, r) for r in range(4)]).astype(jnp.int32)

    def first_kernel(s, xa, ga, xb, gb, up, down):
        part = dot_t(xa[...], ga[...]) + dot_t(xb[...], gb[...])
        up[...] = part[:half].astype(BF16)
        down[...] = part[half:].astype(BF16)

    half_out = jax.ShapeDtypeStruct((half, feats), BF16)
    up, down = call(
        first_kernel,
        scal_w,
        (tokens, value_cotangent, x_other2, g_other),
        [pl.BlockSpec((toks, rows), lambda i, s: (0, s[2])), whole((toks, feats)), whole((toks, rows)), whole((toks, feats))],
        (half_out, half_out),
        (whole((half, feats)), whole((half, feats))),
        4 * toks * rows * feats,
        2 * toks * (2 * rows + 2 * feats) + 2 * rows * feats,
    )
    from_left = send(up, along_x(1))
    from_right = send(down, along_x(-1))

    left1, right1 = ring(weight1)
    top1, bottom1 = ring_on(left1, right1)

    def second_kernel(s, xa1, xa3, xa0, ga, xb, gb, ina, inb, out1, out3, out0):
        g0, g1 = ga[...], gb[...]
        part = dot_t(xa1[...], g0) + dot_t(xb[:, :rows], g1)
        out1[:half] = (part[:half] + ina[...].astype(F32)).astype(BF16)
        out1[half:] = part[half:].astype(BF16)
        part = dot_t(xa3[...], g0) + dot_t(xb[:, rows : 2 * rows], g1)
        out3[:half] = part[:half].astype(BF16)
        out3[half:] = (part[half:] + inb[...].astype(F32)).astype(BF16)
        out0[...] = dot_t(xa0[...], g0) + dot_t(xb[:, 2 * rows :], g1)

    full_out = jax.ShapeDtypeStruct((rows, feats), BF16)
    out1, out3, part0 = call(
        second_kernel,
        scal_w,
        (tokens, tokens, tokens, value_cotangent, x_other130, g_other, from_left, from_right),
        [
            pl.BlockSpec((toks, rows), lambda i, s: (0, s[1])),
            pl.BlockSpec((toks, rows), lambda i, s: (0, s[3])),
            pl.BlockSpec((toks, rows), lambda i, s: (0, s[0])),
            whole((toks, feats)),
            whole((toks, 3 * rows)),
            whole((toks, feats)),
            whole((half, feats)),
            whole((half, feats)),
        ],
        (full_out, full_out, jax.ShapeDtypeStruct((rows, feats), F32)),
        (whole((rows, feats)),) * 3,
        12 * toks * rows * feats,
        2 * toks * (6 * rows + 2 * feats) + 10 * rows * feats,
    )
    sum_left = send(out1, along_x(1))
    sum_right = send(out3, along_x(-1))
    weight_grad = (part0 + sum_left.astype(F32) + sum_right.astype(F32)).astype(BF16)[None]

    def forward(plane, own, left, right, top, bottom, grad_so_far, values_so_far):
        last = values_so_far is not None

        def kernel(s, xr, g, w0, w3, w1, w2a, w2b, *rest):
            if last:
                _, before, grad, vals = rest
            else:
                grad, vals = rest
            total = before[...] if last else jnp.zeros((toks, feats), F32)
            cot = g[...]
            pieces = ((w0, 0, 0), (w3, 3, 0), (w1, 1, 0), (w2a, 2, 0), (w2b, 2, half))
            for ref, r, shift in pieces:
                w = ref[...]
                at = pl.multiple_of(s[1 + r] * rows, 128)
                if shift == 0 and w.shape[0] == rows:
                    total += jnp.dot(xr[:, pl.ds(at, rows)], w, preferred_element_type=F32)
                    grad[:, pl.ds(at, rows)] = lax.dot_general(
                        cot, w, (((1,), (1,)), ((), ())), preferred_element_type=F32
                    ).astype(BF16)
            w = jnp.concatenate([w2a[...], w2b[...]], axis=0)
            at = pl.multiple_of(s[3] * rows, 128)
            total += jnp.dot(xr[:, pl.ds(at, rows)], w, preferred_element_type=F32)
            grad[:, pl.ds(at, rows)] = lax.dot_general(
                cot, w, (((1,), (1,)), ((), ())), preferred_element_type=F32
            ).astype(BF16)
            vals[...] = total.astype(vals.dtype)

        scalars = jnp.stack([plane] + [(x + r) % 4 for r in range(4)]).astype(jnp.int32)
        plane_spec = pl.BlockSpec((toks, 4 * rows), lambda i, s: (0, s[0]))
        operands = [tokens, value_cotangent, own, left, right, top, bottom]
        specs = [plane_spec, whole((toks, feats))] + [whole((rows, feats))] * 3 + [whole((half, feats))] * 2
        aliases = {}
        if last:
            operands += [grad_so_far, values_so_far]
            specs += [pl.BlockSpec(memory_space=pl.ANY), whole((toks, feats))]
            aliases = {8: 0}
        return call(
            kernel,
            scalars,
            operands,
            specs,
            (jax.ShapeDtypeStruct(tokens.shape, BF16), jax.ShapeDtypeStruct((toks, feats), BF16 if last else F32)),
            (plane_spec, whole((toks, feats))),
            16 * toks * rows * feats,
            2 * (8 * toks * rows + 4 * rows * feats + 4 * toks * feats),
            aliases,
        )

    grad, partial_values = forward(y_hi, weight, left0, right0, top0, bottom0, None, None)
    token_grad, values = forward(1 - y_hi, weight1, left1, right1, top1, bottom1, grad, partial_values)

    delta = outer_delta[0]
    quarter = rows // 4
    eighth = rows // 8
    q = y_lo * 2 + core

    def quarter_of(r):
        return lax.dynamic_slice(delta, ((q ^ r) * quarter, 0), (quarter, feats))

    moves = {1: flip(0, 0, 1, 0), 2: flip(1, 0, 0, 0), 3: flip(1, 0, 1, 0)}
    total = quarter_of(0)
    for r in (1, 2, 3):
        total = total + send(quarter_of(r).astype(BF16), moves[r]).astype(F32)
    par = z % 2
    keep = lax.dynamic_slice(total, (par * eighth, 0), (eighth, feats))
    give = lax.dynamic_slice(total, ((1 - par) * eighth, 0), (eighth, feats))
    pair = flip(0, 1, 0, 0)
    total = (keep + send(give.astype(BF16), pair).astype(F32)).astype(BF16)
    up2, down2, far = send(total, along_z(2)), send(total, along_z(-2)), send(total, along_z(4))
    total = ((total.astype(F32) + far.astype(F32)) + (up2.astype(F32) + down2.astype(F32))).astype(BF16)
    other = send(total, pair)
    total = lax.select(
        par == 0, jnp.concatenate([total, other], axis=0), jnp.concatenate([other, total], axis=0)
    )
    parts = [total] + [send(total, moves[r]) for r in (1, 2, 3)]

    def update_kernel(s, a, b, c, d, mom, glob, new_mom, new_glob):
        for r, ref in enumerate((a, b, c, d)):
            here = pl.ds(pl.multiple_of((s[0] ^ r) * quarter, 16), quarter)
            average = ref[...].astype(F32) / jnp.float32(32)
            moment = 0.9 * mom[here] + average
            new_mom[here] = moment
            new_glob[here] = glob[here] - 0.7 * (average + 0.9 * moment)

    state = jax.ShapeDtypeStruct((rows, feats), F32)
    new_momentum, new_global = call(
        update_kernel,
        q.astype(jnp.int32)[None],
        (*parts, momentum, global_weight),
        [whole((quarter, feats))] * 4 + [whole((rows, feats))] * 2,
        (state, state),
        (whole((rows, feats)),) * 2,
        8 * rows * feats,
        18 * rows * feats,
    )
    return (values, token_grad, weight_grad, new_momentum, new_global)


def solution(mesh):
    in_specs = (
        P(("rep", "fsdp"), None),
        P(("rep", "fsdp"), None),
        P("rep", "fsdp", None),
        P("rep", "fsdp", None),
        P("fsdp", None),
        P("fsdp", None),
    )
    out_specs = (
        P(("rep", "fsdp"), None),
        P(("rep", "fsdp"), None),
        P("rep", "fsdp", None),
        P("fsdp", None),
        P("fsdp", None),
    )
    return jax.shard_map(local, mesh=mesh, in_specs=in_specs, out_specs=out_specs, check_vma=False)
```

time: 258 us -> 125 us (0.48)
  the two profiles are of different devices: /device:TPU:1 before, /device:TPU:38 now
where the time goes in v1:
time: 125 us
  waiting for transfers between devices  46.9 us (38%)
  starting transfers between devices  36.4 us (29%)
  local copies, waits for them, and re-layouts  17.7 us (14%)
  Pallas kernels  14.3 us (11%)
  other arithmetic  8.51 us (7%)
    ppermute x26, waiting for transfers between devices, send(): return lax.ppermute(value, AXES, moves)  46.9 us
    ppermute x26, starting transfers between devices, send(): return lax.ppermute(value, AXES, moves)  36.4 us
    pallas_call x5, Pallas kernels, call(): pl.pallas_call(kernel, grid_spec=pltpu.PrefetchScalarGridSpec(num_scalar_...  14.3 us
    unnamed x44, local copies, waits for them, and re-layouts  9.46 us
  transfers between devices with their start and end apart: 26, of which 10 were waited for; matrix products, arithmetic and copies ran while one was open for 12% of the time, Pallas kernels for 8%

profile of v1, /device:TPU:38, one launch (start us, length us, event | category | flops | bytes accessed | tf_op | source)
XLA Modules:
  0.0 124.6 jit_solution(2126427683273527568)
XLA Ops:
  0.7 1.2 fusion.3
  1.9 1.1 collective-permute-start.17
  3.9 3.2 %collective-permute-start = (bf16[640,512]{1,0:T(8,128)(2,1)}, bf16[640,512]{1,0:T(8,128)(2,1)S(1)}, u32[]{:S(2)}, u32[]{:S(2)}) collective-permute-start(bf16[640,512]{1,0:T(8,128)(2,1)} %bitcast.26), channel_id=1, source_target_pairs={{0,4},{1,5},{2,6},{3,7},{4,0},{5,1},{6,2},{7,3},{8,12},{9,13},{10,... | collective-permute-start | bytes 1966088 | tf_op jit(solution)/shard_map/ppermute | solution.py:39
  7.1 2.3 %constant_dynamic-slice_fusion = (bf16[256,640]{1,0:T(8,128)(2,1)S(1)}, bf16[256,640]{1,0:T(8,128)(2,1)}, bf16[256,640]{1,0:T(8,128)(2,1)}, bf16[256,640]{1,0:T(8,128)(2,1)}) fusion(bf16[256,5120]{1,0:T(8,128)(2,1)} %xa0.1, s32[]{:T(128)S(6)} %select_n.114, s32[]{:T(128)S(6)} %select_n.113, s32[]{:T(128)S(6)} %select_n.112, s32[]{:T(128)S(6)} %select_n.111), kind=kLoop, calls=%fused_computation.17 | loop fusion | bytes 2621456 | tf_op jit(solution)/shard_map/dynamic_slice | solution.py:86
  9.3 2.8 %collective-permute-done.16 = bf16[160,512]{1,0:T(8,128)(2,1)S(1)} collective-permute-done((bf16[160,512]{1,0:T(8,128)(2,1)S(1)}, bf16[160,512]{1,0:T(8,128)(2,1)S(1)}, u32[]{:S(2)}, u32[]{:S(2)}) %collective-permute-start.16) | collective-permute-done | bytes 163872 | tf_op jit(solution)/shard_map/ppermute | solution.py:39
  14.3 3.1 %collective-permute-start.10 = (bf16[256,1152]{1,0:T(8,128)(2,1)}, bf16[256,1152]{1,0:T(8,128)(2,1)}, u32[]{:S(2)}, u32[]{:S(2)}) collective-permute-start(bf16[256,1152]{1,0:T(8,128)(2,1)} %pad_maximum_fusion.1), channel_id=1, source_target_pairs={{0,4},{1,5},{2,6},{3,7},{4,0},{5,1},{6,2},{7,3},{8,12},{9,13},{10,... | collective-permute-start | bytes 1769480 | tf_op jit(solution)/shard_map/ppermute | solution.py:39
  18.4 5.9 %collective-permute-start.21 = (bf16[80,512]{1,0:T(8,128)(2,1)}, bf16[80,512]{1,0:T(8,128)(2,1)}, u32[]{:S(2)}, u32[]{:S(2)}) collective-permute-start(bf16[80,512]{1,0:T(8,128)(2,1)} %add_convert_fusion.2), channel_id=1, source_target_pairs={{0,96},{1,97},{2,98},{3,99},{4,100},{5,101},{6,102},{7,103},{8,104... | collective-permute-start | bytes 245768 | tf_op jit(solution)/shard_map/ppermute | solution.py:39
  24.3 3.8 %collective-permute-start.19 = (bf16[80,512]{1,0:T(8,128)(2,1)}, bf16[80,512]{1,0:T(8,128)(2,1)}, u32[]{:S(2)}, u32[]{:S(2)}) collective-permute-start(bf16[80,512]{1,0:T(8,128)(2,1)} %add_convert_fusion.2), channel_id=1, source_target_pairs={{0,64},{1,65},{2,66},{3,67},{4,68},{5,69},{6,70},{7,71},{8,72},{9,... | collective-permute-start | bytes 245768 | tf_op jit(solution)/shard_map/ppermute | solution.py:39
  28.1 2.3 %pad_maximum_fusion = bf16[256,1920]{1,0:T(8,128)(2,1)} fusion(bf16[256,640]{1,0:T(8,128)(2,1)} %get-tuple-element.28, bf16[256,640]{1,0:T(8,128)(2,1)} %get-tuple-element.29, bf16[256,640]{1,0:T(8,128)(2,1)} %get-tuple-element.30), kind=kLoop, calls=%fused_computation.1 | loop fusion | flops 2949120 | bytes 1966080 | tf_op jit(solution)/shard_map/concatenate | solution.py:96
  30.5 2.6 %collective-permute-start.9 = (bf16[256,1920]{1,0:T(8,128)(2,1)}, bf16[256,1920]{1,0:T(8,128)(2,1)S(1)}, u32[]{:S(2)}, u32[]{:S(2)}) collective-permute-start(bf16[256,1920]{1,0:T(8,128)(2,1)} %pad_maximum_fusion), channel_id=1, source_target_pairs={{0,4},{1,5},{2,6},{3,7},{4,0},{5,1},{6,2},{7,3},{8,12},{9,13},{10,... | collective-permute-start | bytes 2949128 | tf_op jit(solution)/shard_map/ppermute | solution.py:39
  33.0 2.7 %collective-permute-done.20 = bf16[80,512]{1,0:T(8,128)(2,1)} collective-permute-done((bf16[80,512]{1,0:T(8,128)(2,1)}, bf16[80,512]{1,0:T(8,128)(2,1)}, u32[]{:S(2)}, u32[]{:S(2)}) %collective-permute-start.20) | collective-permute-done | bytes 81952 | tf_op jit(solution)/shard_map/ppermute | solution.py:39
  37.0 4.3 %collective-permute-done.22 = bf16[80,512]{1,0:T(8,128)(2,1)S(1)} collective-permute-done((bf16[80,512]{1,0:T(8,128)(2,1)S(1)}, bf16[80,512]{1,0:T(8,128)(2,1)S(1)}, u32[]{:S(2)}, u32[]{:S(2)}) %collective-permute-start.22) | collective-permute-done | bytes 81952 | tf_op jit(solution)/shard_map/ppermute | solution.py:39
  45.1 1.5 %collective-permute-start.5 = (bf16[640,512]{1,0:T(8,128)(2,1)S(1)}, bf16[640,512]{1,0:T(8,128)(2,1)S(1)}, u32[]{:S(2)}, u32[]{:S(2)}) collective-permute-start(bf16[640,512]{1,0:T(8,128)(2,1)S(1)} %bitcast.27), channel_id=1, source_target_pairs={{0,1},{1,2},{2,3},{3,0},{4,5},{5,6},{6,7},{7,4},{8,9},{9,10},{10,1... | collective-permute-start | bytes 1966088 | tf_op jit(solution)/shard_map/ppermute | solution.py:39
  47.8 1.5 %collective-permute-start.12 = (bf16[320,512]{1,0:T(8,128)(2,1)S(1)}, bf16[320,512]{1,0:T(8,128)(2,1)S(1)}, u32[]{:S(2)}, u32[]{:S(2)}) collective-permute-start(bf16[320,512]{1,0:T(8,128)(2,1)S(1)} %get-tuple-element.21), channel_id=1, source_target_pairs={{0,3},{1,0},{2,1},{3,2},{4,7},{5,4},{6,5},{7,6},{8,11},{9,8},{10,9... | collective-permute-start | bytes 983048 | tf_op jit(solution)/shard_map/ppermute | solution.py:39
  49.4 5.8 %collective-permute-done.11.ina = bf16[320,512]{1,0:T(8,128)(2,1)S(1)} collective-permute-done((bf16[320,512]{1,0:T(8,128)(2,1)S(1)}, bf16[320,512]{1,0:T(8,128)(2,1)S(1)}, u32[]{:S(2)}, u32[]{:S(2)}) %collective-permute-start.11) | collective-permute-done | bytes 327712 | tf_op jit(solution)/shard_map/ppermute | solution.py:39
  55.2 1.7 %collective-permute-start.1 = (bf16[640,512]{1,0:T(8,128)(2,1)}, bf16[640,512]{1,0:T(8,128)(2,1)S(1)}, u32[]{:S(2)}, u32[]{:S(2)}) collective-permute-start(bf16[640,512]{1,0:T(8,128)(2,1)} %copy-done.10), channel_id=1, source_target_pairs={{0,1},{1,2},{2,3},{3,0},{4,5},{5,6},{6,7},{7,4},{8,9},{9,10},{10,1... | collective-permute-start | bytes 1966088 | tf_op jit(solution)/shard_map/ppermute | solution.py:39
  56.9 15.2 %collective-permute-done.12.inb = bf16[320,512]{1,0:T(8,128)(2,1)S(1)} collective-permute-done((bf16[320,512]{1,0:T(8,128)(2,1)S(1)}, bf16[320,512]{1,0:T(8,128)(2,1)S(1)}, u32[]{:S(2)}, u32[]{:S(2)}) %collective-permute-start.12) | collective-permute-done | bytes 327712 | tf_op jit(solution)/shard_map/ppermute | solution.py:39
  72.9 2.3 %shard_map.104 = (bf16[640,512]{1,0:T(8,128)(2,1)}, bf16[640,512]{1,0:T(8,128)(2,1)}, f32[640,512]{1,0:T(8,128)S(1)}) custom-call(s32[4]{0:T(128)S(1)} %pad_add_fusion.s, bf16[256,5120]{1,0:T(8,128)(2,1)S(1)} %copy-done, bf16[256,5120]{1,0:T(8,128)(2,1)S(1)} %copy-done, bf16[256,5120]{1,0:T(8,128)(2,1)S(1)} %copy-done, bf16[256,512]{1,0:T(8,128)(2,1)S(1)} %copy-done.1, ...), custom_call_target="tpu_custom_call" | custom-call | flops 1006632960 | bytes 5767168 | tf_op jit(solution)/shard_map/pallas_call | solution.py:51
  75.2 1.1 copy-done.6
  76.3 1.1 collective-permute-done.24.c
  78.1 3.2 %collective-permute-start.13 = (bf16[640,512]{1,0:T(8,128)(2,1)}, bf16[640,512]{1,0:T(8,128)(2,1)}, u32[]{:S(2)}, u32[]{:S(2)}) collective-permute-start(bf16[640,512]{1,0:T(8,128)(2,1)} %get-tuple-element.23), channel_id=1, source_target_pairs={{0,1},{1,2},{2,3},{3,0},{4,5},{5,6},{6,7},{7,4},{8,9},{9,10},{10,1... | collective-permute-start | bytes 1966088 | tf_op jit(solution)/shard_map/ppermute | solution.py:39
  83.0 4.2 %collective-permute-done.25.d = bf16[160,512]{1,0:T(8,128)(2,1)S(1)} collective-permute-done((bf16[160,512]{1,0:T(8,128)(2,1)S(1)}, bf16[160,512]{1,0:T(8,128)(2,1)S(1)}, u32[]{:S(2)}, u32[]{:S(2)}) %collective-permute-start.25) | collective-permute-done | bytes 163872 | tf_op jit(solution)/shard_map/ppermute | solution.py:39
  87.9 1.4 %collective-permute-start.7 = (bf16[320,512]{1,0:T(8,128)(2,1)}, bf16[320,512]{1,0:T(8,128)(2,1)}, u32[]{:S(2)}, u32[]{:S(2)}) collective-permute-start(bf16[320,512]{1,0:T(8,128)(2,1)} %slice.26), channel_id=1, source_target_pairs={{0,1},{1,2},{2,3},{3,0},{4,5},{5,6},{6,7},{7,4},{8,9},{9,10},{10,1... | collective-permute-start | bytes 983048 | tf_op jit(solution)/shard_map/ppermute | solution.py:39
  90.1 1.3 %copy-done.8 = f32[640,512]{1,0:T(8,128)S(1)} copy-done((f32[640,512]{1,0:T(8,128)S(1)}, f32[640,512]{1,0:T(8,128)}, u32[]{:S(2)}) %copy-start.8) | copy-done | bytes 1310744
  91.4 1.3 %copy-done.9 = f32[640,512]{1,0:T(8,128)S(1)} copy-done((f32[640,512]{1,0:T(8,128)S(1)}, f32[640,512]{1,0:T(8,128)}, u32[]{:S(2)}) %copy-start.9) | copy-done | bytes 1310744
  96.4 1.9 %shard_map.105 = (f32[640,512]{1,0:T(8,128)}, f32[640,512]{1,0:T(8,128)}) custom-call(s32[1]{0:T(128)} %bitcast.12.s, bf16[160,512]{1,0:T(8,128)(2,1)S(1)} %copy-done.13, bf16[160,512]{1,0:T(8,128)(2,1)S(1)} %copy-done.17, bf16[160,512]{1,0:T(8,128)(2,1)S(1)} %copy-done.19, bf16[160,512]{1,0:T(8,128)(2,1)S(1)} %copy-done.21, f32[640,512]{1,0:T(8,128)S(1)} %copy-done.8, ...), custom_call_target="tpu_custom_call" | custom-call | flops 2621440 | bytes 5898240 | tf_op jit(solution)/shard_map/pallas_call | solution.py:51
  98.3 2.7 %collective-permute-start.3 = (bf16[320,512]{1,0:T(8,128)(2,1)S(1)}, bf16[320,512]{1,0:T(8,128)(2,1)S(1)}, u32[]{:S(2)}, u32[]{:S(2)}) collective-permute-start(bf16[320,512]{1,0:T(8,128)(2,1)S(1)} %slice.24), channel_id=1, source_target_pairs={{0,1},{1,2},{2,3},{3,0},{4,5},{5,6},{6,7},{7,4},{8,9},{9,10},{10,1... | collective-permute-start | bytes 983048 | tf_op jit(solution)/shard_map/ppermute | solution.py:39
  102.0 2.4 %collective-permute-done.7.w2a = bf16[320,512]{1,0:T(8,128)(2,1)} collective-permute-done((bf16[320,512]{1,0:T(8,128)(2,1)}, bf16[320,512]{1,0:T(8,128)(2,1)}, u32[]{:S(2)}, u32[]{:S(2)}) %collective-permute-start.7) | collective-permute-done | bytes 327712 | tf_op jit(solution)/shard_map/ppermute | solution.py:39
  105.2 7.9 %collective-permute-done.8.w2b = bf16[320,512]{1,0:T(8,128)(2,1)} collective-permute-done((bf16[320,512]{1,0:T(8,128)(2,1)}, bf16[320,512]{1,0:T(8,128)(2,1)}, u32[]{:S(2)}, u32[]{:S(2)}) %collective-permute-start.8) | collective-permute-done | bytes 327712 | tf_op jit(solution)/shard_map/ppermute | solution.py:39
  113.1 4.5 %shard_map.101 = (bf16[256,5120]{1,0:T(8,128)(2,1)}, f32[256,512]{1,0:T(8,128)S(1)}) custom-call(s32[5]{0:T(128)S(1)} %stack.50.s, bf16[256,5120]{1,0:T(8,128)(2,1)S(1)} %copy-done, bf16[256,512]{1,0:T(8,128)(2,1)S(1)} %copy-done.1, bf16[640,512]{1,0:T(8,128)(2,1)S(1)} %bitcast.29, bf16[640,512]{1,0:T(8,128)(2,1)S(1)} %copy-done.3, ...), custom_call_target="tpu_custom_call" | custom-call | flops 1342177280 | bytes 6291456 | tf_op jit(solution)/shard_map/pallas_call | solution.py:51
  117.7 2.5 %fusion = bf16[1,640,512]{2,1,0:T(8,128)(2,1)} fusion(bf16[640,512]{1,0:T(8,128)(2,1)} %collective-permute-done.14, f32[640,512]{1,0:T(8,128)S(1)} %copy-done.7, bf16[640,512]{1,0:T(8,128)(2,1)} %collective-permute-done.13), kind=kLoop, calls=%fused_computation.2 | loop fusion | flops 1638400 | bytes 3276800 | tf_op jit(solution)/shard_map/broadcast_in_dim | solution.py:159
  120.1 4.5 %shard_map.102 = (bf16[256,5120]{1,0:T(8,128)(2,1)}, bf16[256,512]{1,0:T(8,128)(2,1)}) custom-call(s32[5]{0:T(128)S(1)} %stack.48.s, bf16[256,5120]{1,0:T(8,128)(2,1)S(1)} %copy-done, bf16[256,512]{1,0:T(8,128)(2,1)S(1)} %copy-done.1, bf16[640,512]{1,0:T(8,128)(2,1)S(1)} %copy-done.11, ...), custom_call_target="tpu_custom_call", output_to_operand_aliasing={{0}: (8, {})} | custom-call | flops 1342177280 | bytes 6291456 | tf_op jit(solution)/shard_map/pallas_call | solution.py:51
  (88 shorter events, 20.3 us)
Async XLA Ops:
  1.9 7.4 %collective-permute-start.17 = (bf16[160,512]{1,0:T(8,128)(2,1)S(1)}, bf16[160,512]{1,0:T(8,128)(2,1)S(1)}, u32[]{:S(2)}, u32[]{:S(2)}) collective-permute-start(bf16[160,512]{1,0:T(8,128)(2,1)S(1)} %get-tuple-element.32), channel_id=1, source_target_pairs={{0,136},{1,137},{2,138},{3,139},{4,140},{5,141},{6,142},{7,143},{8... | collective-permute-start | bytes 491528 | tf_op jit(solution)/shard_map/ppermute | solution.py:39
  3.0 9.1 %collective-permute-start.16 = (bf16[160,512]{1,0:T(8,128)(2,1)S(1)}, bf16[160,512]{1,0:T(8,128)(2,1)S(1)}, u32[]{:S(2)}, u32[]{:S(2)}) collective-permute-start(bf16[160,512]{1,0:T(8,128)(2,1)S(1)} %get-tuple-element.33), channel_id=1, source_target_pairs={{0,128},{1,129},{2,130},{3,131},{4,132},{5,133},{6,134},{7,135},{8... | collective-permute-start | bytes 491528 | tf_op jit(solution)/shard_map/ppermute | solution.py:39
  3.7 8.5 %collective-permute-start.15 = (bf16[160,512]{1,0:T(8,128)(2,1)S(1)}, bf16[160,512]{1,0:T(8,128)(2,1)S(1)}, u32[]{:S(2)}, u32[]{:S(2)}) collective-permute-start(bf16[160,512]{1,0:T(8,128)(2,1)S(1)} %get-tuple-element.31), channel_id=1, source_target_pairs={{0,8},{1,9},{2,10},{3,11},{4,12},{5,13},{6,14},{7,15},{8,0},{9,1},... | collective-permute-start | bytes 491528 | tf_op jit(solution)/shard_map/ppermute | solution.py:39
  3.9 44.0 %collective-permute-start = (bf16[640,512]{1,0:T(8,128)(2,1)}, bf16[640,512]{1,0:T(8,128)(2,1)S(1)}, u32[]{:S(2)}, u32[]{:S(2)}) collective-permute-start(bf16[640,512]{1,0:T(8,128)(2,1)} %bitcast.26), channel_id=1, source_target_pairs={{0,4},{1,5},{2,6},{3,7},{4,0},{5,1},{6,2},{7,3},{8,12},{9,13},{10,... | collective-permute-start | bytes 1966088 | tf_op jit(solution)/shard_map/ppermute | solution.py:39
  13.2 4.5 %collective-permute-start.18 = (bf16[80,512]{1,0:T(8,128)(2,1)S(1)}, bf16[80,512]{1,0:T(8,128)(2,1)S(1)}, u32[]{:S(2)}, u32[]{:S(2)}) collective-permute-start(bf16[80,512]{1,0:T(8,128)(2,1)S(1)} %dynamic-slice_convert_fusion.3), channel_id=1, source_target_pairs={{0,16},{1,17},{2,18},{3,19},{4,20},{5,21},{6,22},{7,23},{8,24},{9,... | collective-permute-start | bytes 245768 | tf_op jit(solution)/shard_map/ppermute | solution.py:39
  14.3 27.2 %collective-permute-start.10 = (bf16[256,1152]{1,0:T(8,128)(2,1)}, bf16[256,1152]{1,0:T(8,128)(2,1)}, u32[]{:S(2)}, u32[]{:S(2)}) collective-permute-start(bf16[256,1152]{1,0:T(8,128)(2,1)} %pad_maximum_fusion.1), channel_id=1, source_target_pairs={{0,4},{1,5},{2,6},{3,7},{4,0},{5,1},{6,2},{7,3},{8,12},{9,13},{10,... | collective-permute-start | bytes 1769480 | tf_op jit(solution)/shard_map/ppermute | solution.py:39
  18.4 12.1 %collective-permute-start.21 = (bf16[80,512]{1,0:T(8,128)(2,1)}, bf16[80,512]{1,0:T(8,128)(2,1)}, u32[]{:S(2)}, u32[]{:S(2)}) collective-permute-start(bf16[80,512]{1,0:T(8,128)(2,1)} %add_convert_fusion.2), channel_id=1, source_target_pairs={{0,96},{1,97},{2,98},{3,99},{4,100},{5,101},{6,102},{7,103},{8,104... | collective-permute-start | bytes 245768 | tf_op jit(solution)/shard_map/ppermute | solution.py:39
  24.3 11.4 %collective-permute-start.20 = (bf16[80,512]{1,0:T(8,128)(2,1)}, bf16[80,512]{1,0:T(8,128)(2,1)}, u32[]{:S(2)}, u32[]{:S(2)}) collective-permute-start(bf16[80,512]{1,0:T(8,128)(2,1)} %add_convert_fusion.2), channel_id=1, source_target_pairs={{0,32},{1,33},{2,34},{3,35},{4,36},{5,37},{6,38},{7,39},{8,40},{9,... | collective-permute-start | bytes 245768 | tf_op jit(solution)/shard_map/ppermute | solution.py:39
  24.3 11.4 %collective-permute-start.19 = (bf16[80,512]{1,0:T(8,128)(2,1)}, bf16[80,512]{1,0:T(8,128)(2,1)}, u32[]{:S(2)}, u32[]{:S(2)}) collective-permute-start(bf16[80,512]{1,0:T(8,128)(2,1)} %add_convert_fusion.2), channel_id=1, source_target_pairs={{0,64},{1,65},{2,66},{3,67},{4,68},{5,69},{6,70},{7,71},{8,72},{9,... | collective-permute-start | bytes 245768 | tf_op jit(solution)/shard_map/ppermute | solution.py:39
  28.1 15.3 %copy-start = (bf16[256,5120]{1,0:T(8,128)(2,1)S(1)}, bf16[256,5120]{1,0:T(8,128)(2,1)}, u32[]{:S(2)}) copy-start(bf16[256,5120]{1,0:T(8,128)(2,1)} %xa0.1) | copy-start | bytes 7864324
  30.5 42.4 %collective-permute-start.9 = (bf16[256,1920]{1,0:T(8,128)(2,1)}, bf16[256,1920]{1,0:T(8,128)(2,1)S(1)}, u32[]{:S(2)}, u32[]{:S(2)}) collective-permute-start(bf16[256,1920]{1,0:T(8,128)(2,1)} %pad_maximum_fusion), channel_id=1, source_target_pairs={{0,4},{1,5},{2,6},{3,7},{4,0},{5,1},{6,2},{7,3},{8,12},{9,13},{10,... | collective-permute-start | bytes 2949128 | tf_op jit(solution)/shard_map/ppermute | solution.py:39
  36.8 4.5 %collective-permute-start.22 = (bf16[80,512]{1,0:T(8,128)(2,1)S(1)}, bf16[80,512]{1,0:T(8,128)(2,1)S(1)}, u32[]{:S(2)}, u32[]{:S(2)}) collective-permute-start(bf16[80,512]{1,0:T(8,128)(2,1)S(1)} %add_convert_fusion.1), channel_id=1, source_target_pairs={{0,16},{1,17},{2,18},{3,19},{4,20},{5,21},{6,22},{7,23},{8,24},{9,... | collective-permute-start | bytes 245768 | tf_op jit(solution)/shard_map/ppermute | solution.py:39
  41.4 40.0 %copy-start.12 = (bf16[160,512]{1,0:T(8,128)(2,1)}, bf16[160,512]{1,0:T(8,128)(2,1)S(1)}, u32[]{:S(2)}) copy-start(bf16[160,512]{1,0:T(8,128)(2,1)S(1)} %maximum_select_fusion.a) | copy-start | bytes 491524
  41.4 5.3 %collective-permute-start.23 = (bf16[160,512]{1,0:T(8,128)(2,1)S(1)}, bf16[160,512]{1,0:T(8,128)(2,1)S(1)}, u32[]{:S(2)}, u32[]{:S(2)}) collective-permute-start(bf16[160,512]{1,0:T(8,128)(2,1)S(1)} %maximum_select_fusion.a), channel_id=1, source_target_pairs={{0,8},{1,9},{2,10},{3,11},{4,12},{5,13},{6,14},{7,15},{8,0},{9,1},... | collective-permute-start | bytes 491528 | tf_op jit(solution)/shard_map/ppermute | solution.py:39
  44.6 10.6 %collective-permute-start.11 = (bf16[320,512]{1,0:T(8,128)(2,1)S(1)}, bf16[320,512]{1,0:T(8,128)(2,1)S(1)}, u32[]{:S(2)}, u32[]{:S(2)}) collective-permute-start(bf16[320,512]{1,0:T(8,128)(2,1)S(1)} %get-tuple-element.20), channel_id=1, source_target_pairs={{0,1},{1,2},{2,3},{3,0},{4,5},{5,6},{6,7},{7,4},{8,9},{9,10},{10,1... | collective-permute-start | bytes 983048 | tf_op jit(solution)/shard_map/ppermute | solution.py:39
  45.1 32.9 %collective-permute-start.5 = (bf16[640,512]{1,0:T(8,128)(2,1)S(1)}, bf16[640,512]{1,0:T(8,128)(2,1)S(1)}, u32[]{:S(2)}, u32[]{:S(2)}) collective-permute-start(bf16[640,512]{1,0:T(8,128)(2,1)S(1)} %bitcast.27), channel_id=1, source_target_pairs={{0,1},{1,2},{2,3},{3,0},{4,5},{5,6},{6,7},{7,4},{8,9},{9,10},{10,1... | collective-permute-start | bytes 1966088 | tf_op jit(solution)/shard_map/ppermute | solution.py:39
  47.3 34.0 %collective-permute-start.6 = (bf16[640,512]{1,0:T(8,128)(2,1)S(1)}, bf16[640,512]{1,0:T(8,128)(2,1)S(1)}, u32[]{:S(2)}, u32[]{:S(2)}) collective-permute-start(bf16[640,512]{1,0:T(8,128)(2,1)S(1)} %bitcast.28), channel_id=1, source_target_pairs={{0,3},{1,0},{2,1},{3,2},{4,7},{5,4},{6,5},{7,6},{8,11},{9,8},{10,9... | collective-permute-start | bytes 1966088 | tf_op jit(solution)/shard_map/ppermute | solution.py:39
  47.8 24.3 %collective-permute-start.12 = (bf16[320,512]{1,0:T(8,128)(2,1)S(1)}, bf16[320,512]{1,0:T(8,128)(2,1)S(1)}, u32[]{:S(2)}, u32[]{:S(2)}) collective-permute-start(bf16[320,512]{1,0:T(8,128)(2,1)S(1)} %get-tuple-element.21), channel_id=1, source_target_pairs={{0,3},{1,0},{2,1},{3,2},{4,7},{5,4},{6,5},{7,6},{8,11},{9,8},{10,9... | collective-permute-start | bytes 983048 | tf_op jit(solution)/shard_map/ppermute | solution.py:39
  55.2 34.1 %collective-permute-start.1 = (bf16[640,512]{1,0:T(8,128)(2,1)}, bf16[640,512]{1,0:T(8,128)(2,1)S(1)}, u32[]{:S(2)}, u32[]{:S(2)}) collective-permute-start(bf16[640,512]{1,0:T(8,128)(2,1)} %copy-done.10), channel_id=1, source_target_pairs={{0,1},{1,2},{2,3},{3,0},{4,5},{5,6},{6,7},{7,4},{8,9},{9,10},{10,1... | collective-permute-start | bytes 1966088 | tf_op jit(solution)/shard_map/ppermute | solution.py:39
  72.1 5.3 %collective-permute-start.24 = (bf16[160,512]{1,0:T(8,128)(2,1)S(1)}, bf16[160,512]{1,0:T(8,128)(2,1)S(1)}, u32[]{:S(2)}, u32[]{:S(2)}) collective-permute-start(bf16[160,512]{1,0:T(8,128)(2,1)S(1)} %maximum_select_fusion.a), channel_id=1, source_target_pairs={{0,128},{1,129},{2,130},{3,131},{4,132},{5,133},{6,134},{7,135},{8... | collective-permute-start | bytes 491528 | tf_op jit(solution)/shard_map/ppermute | solution.py:39
  72.9 25.4 %collective-permute-start.2 = (bf16[640,512]{1,0:T(8,128)(2,1)}, bf16[640,512]{1,0:T(8,128)(2,1)}, u32[]{:S(2)}, u32[]{:S(2)}) collective-permute-start(bf16[640,512]{1,0:T(8,128)(2,1)} %copy-done.10), channel_id=1, source_target_pairs={{0,3},{1,0},{2,1},{3,2},{4,7},{5,4},{6,5},{7,6},{8,11},{9,8},{10,9... | collective-permute-start | bytes 1966088 | tf_op jit(solution)/shard_map/ppermute | solution.py:39
  78.1 39.6 %collective-permute-start.14 = (bf16[640,512]{1,0:T(8,128)(2,1)}, bf16[640,512]{1,0:T(8,128)(2,1)}, u32[]{:S(2)}, u32[]{:S(2)}) collective-permute-start(bf16[640,512]{1,0:T(8,128)(2,1)} %get-tuple-element.24), channel_id=1, source_target_pairs={{0,3},{1,0},{2,1},{3,2},{4,7},{5,4},{6,5},{7,6},{8,11},{9,8},{10,9... | collective-permute-start | bytes 1966088 | tf_op jit(solution)/shard_map/ppermute | solution.py:39
  78.1 39.6 %collective-permute-start.13 = (bf16[640,512]{1,0:T(8,128)(2,1)}, bf16[640,512]{1,0:T(8,128)(2,1)}, u32[]{:S(2)}, u32[]{:S(2)}) collective-permute-start(bf16[640,512]{1,0:T(8,128)(2,1)} %get-tuple-element.23), channel_id=1, source_target_pairs={{0,1},{1,2},{2,3},{3,0},{4,5},{5,6},{6,7},{7,4},{8,9},{9,10},{10,1... | collective-permute-start | bytes 1966088 | tf_op jit(solution)/shard_map/ppermute | solution.py:39
  81.3 5.9 %collective-permute-start.25 = (bf16[160,512]{1,0:T(8,128)(2,1)S(1)}, bf16[160,512]{1,0:T(8,128)(2,1)S(1)}, u32[]{:S(2)}, u32[]{:S(2)}) collective-permute-start(bf16[160,512]{1,0:T(8,128)(2,1)S(1)} %maximum_select_fusion.a), channel_id=1, source_target_pairs={{0,136},{1,137},{2,138},{3,139},{4,140},{5,141},{6,142},{7,143},{8... | collective-permute-start | bytes 491528 | tf_op jit(solution)/shard_map/ppermute | solution.py:39
  87.9 16.5 %collective-permute-start.7 = (bf16[320,512]{1,0:T(8,128)(2,1)}, bf16[320,512]{1,0:T(8,128)(2,1)}, u32[]{:S(2)}, u32[]{:S(2)}) collective-permute-start(bf16[320,512]{1,0:T(8,128)(2,1)} %slice.26), channel_id=1, source_target_pairs={{0,1},{1,2},{2,3},{3,0},{4,5},{5,6},{6,7},{7,4},{8,9},{9,10},{10,1... | collective-permute-start | bytes 983048 | tf_op jit(solution)/shard_map/ppermute | solution.py:39
  89.3 23.8 %collective-permute-start.8 = (bf16[320,512]{1,0:T(8,128)(2,1)}, bf16[320,512]{1,0:T(8,128)(2,1)}, u32[]{:S(2)}, u32[]{:S(2)}) collective-permute-start(bf16[320,512]{1,0:T(8,128)(2,1)} %slice.27), channel_id=1, source_target_pairs={{0,3},{1,0},{2,1},{3,2},{4,7},{5,4},{6,5},{7,6},{8,11},{9,8},{10,9... | collective-permute-start | bytes 983048 | tf_op jit(solution)/shard_map/ppermute | solution.py:39
  96.4 16.7 %copy-start.15 = (bf16[1,640,512]{2,1,0:T(8,128)(2,1)S(1)}, bf16[1,640,512]{2,1,0:T(8,128)(2,1)}, u32[]{:S(2)}) copy-start(bf16[1,640,512]{2,1,0:T(8,128)(2,1)} %param.8) | copy-start | bytes 1966084
  98.3 14.9 %copy-start.3 = (bf16[640,512]{1,0:T(8,128)(2,1)S(1)}, bf16[640,512]{1,0:T(8,128)(2,1)}, u32[]{:S(2)}) copy-start(bf16[640,512]{1,0:T(8,128)(2,1)} %copy-done.2) | copy-start | bytes 1966084
  98.3 14.9 %copy-start.5 = (bf16[640,512]{1,0:T(8,128)(2,1)S(1)}, bf16[640,512]{1,0:T(8,128)(2,1)}, u32[]{:S(2)}) copy-start(bf16[640,512]{1,0:T(8,128)(2,1)} %copy-done.4) | copy-start | bytes 1966084
  98.3 21.8 %collective-permute-start.3 = (bf16[320,512]{1,0:T(8,128)(2,1)S(1)}, bf16[320,512]{1,0:T(8,128)(2,1)S(1)}, u32[]{:S(2)}, u32[]{:S(2)}) collective-permute-start(bf16[320,512]{1,0:T(8,128)(2,1)S(1)} %slice.24), channel_id=1, source_target_pairs={{0,1},{1,2},{2,3},{3,0},{4,5},{5,6},{6,7},{7,4},{8,9},{9,10},{10,1... | collective-permute-start | bytes 983048 | tf_op jit(solution)/shard_map/ppermute | solution.py:39
  102.0 15.6 %copy-start.7 = (f32[640,512]{1,0:T(8,128)S(1)}, f32[640,512]{1,0:T(8,128)}, u32[]{:S(2)}) copy-start(f32[640,512]{1,0:T(8,128)} %copy-done.6) | copy-start | bytes 3932164
  104.4 15.7 %collective-permute-start.4 = (bf16[320,512]{1,0:T(8,128)(2,1)S(1)}, bf16[320,512]{1,0:T(8,128)(2,1)S(1)}, u32[]{:S(2)}, u32[]{:S(2)}) collective-permute-start(bf16[320,512]{1,0:T(8,128)(2,1)S(1)} %slice.25), channel_id=1, source_target_pairs={{0,3},{1,0},{2,1},{3,2},{4,7},{5,4},{6,5},{7,6},{8,11},{9,8},{10,9... | collective-permute-start | bytes 983048 | tf_op jit(solution)/shard_map/ppermute | solution.py:39
  (16 other events, 39.0 us)

commit v2 on v0

v2 whole, which is shorter than its diff:
```python
import itertools

import jax
import jax.numpy as jnp
from jax import lax
from jax.experimental import pallas as pl
from jax.experimental.pallas import tpu as pltpu
from jax.sharding import PartitionSpec as P

AXES = ("rep", "fsdp")
GRID = (2, 8, 2, 2, 4)
F32, BF16 = jnp.float32, jnp.bfloat16


def flat(place):
    index = 0
    for coordinate, size in zip(place, GRID):
        index = index * size + coordinate % size
    return index


def permutation(move):
    return [(flat(c), flat(move(*c))) for c in itertools.product(*map(range, GRID))]


def along_x(step):
    return permutation(lambda l, z, c, h, x: (l, z, c, h, x + step))


def along_z(step):
    return permutation(lambda l, z, c, h, x: (l, z + step, c, h, x))


def flip(dl, dz, dc, dh):
    return permutation(lambda l, z, c, h, x: (l ^ dl, z ^ dz, c ^ dc, h ^ dh, x))


def send(value, moves):
    return lax.ppermute(value, AXES, moves)


def after(value, *others):
    return lax.optimization_barrier((value, *others))[0]


def dot_t(a, b):
    return lax.dot_general(a, b, (((0,), (0,)), ((), ())), preferred_element_type=F32)


def whole(shape):
    return pl.BlockSpec(shape, lambda i, s: (0,) * len(shape))


def call(kernel, scalars, operands, specs, outs, out_specs, flops, moved, aliases={}, scratch=()):
    return pl.pallas_call(
        kernel,
        grid_spec=pltpu.PrefetchScalarGridSpec(
            num_scalar_prefetch=1, grid=(1,), in_specs=specs, out_specs=out_specs, scratch_shapes=scratch
        ),
        out_shape=outs,
        input_output_aliases=aliases,
        cost_estimate=pl.CostEstimate(flops=flops, bytes_accessed=moved, transcendentals=0),
        compiler_params=pltpu.CompilerParams(vmem_limit_bytes=32 * 2**20),
    )(scalars, *operands)


def local(tokens, value_cotangent, value_weight, outer_delta, momentum, global_weight):
    rep, fsdp = lax.axis_index("rep"), lax.axis_index("fsdp")
    y_lo, z, core = rep // 16, (rep // 2) % 8, rep % 2
    y_hi, x = fsdp // 4, fsdp % 4
    rows, feats = value_weight.shape[1:]
    toks = tokens.shape[0]
    half = rows // 2
    weight = value_weight[0]

    def ring(own):
        return send(own, right_on), send(own, left_on)


    def column(plane, r):
        return plane * 4 + (x + r) % 4

    def block_for_partner(r):
        return lax.dynamic_slice(tokens, (0, column(1 - y_hi, r) * rows), (toks, rows))

    across = flip(0, 0, 0, 1)
    right_on, left_on = along_x(1), along_x(-1)

    left0, right0 = send(weight, right_on), send(weight, left_on)
    weight1 = send(weight, across)

    delta = outer_delta[0]
    halves, quarter = rows // 2, rows // 4
    pair_c, pair_l, pair_z = flip(0, 0, 1, 0), flip(1, 0, 0, 0), flip(0, 1, 0, 0)
    mine = lax.dynamic_slice(delta, (core * halves, 0), (halves, feats))
    give = lax.dynamic_slice(delta, ((1 - core) * halves, 0), (halves, feats)).astype(BF16)
    total = mine + send(give, pair_c).astype(F32)
    bit = z % 2
    give = lax.dynamic_slice(total, ((1 - bit) * quarter, 0), (quarter, feats)).astype(BF16)
    total = lax.dynamic_slice(total, (bit * quarter, 0), (quarter, feats))
    total = (total + send(give, pair_z).astype(F32)).astype(BF16)

    def pack_kernel(s, x2, x1, x3, x0, cot, one, two):
        one[:, :rows] = x2[...]
        one[:, rows:] = cot[...]
        two[:, :rows] = x1[...]
        two[:, rows : 2 * rows] = x3[...]
        two[:, 2 * rows :] = x0[...]

    def block_of(k):
        return pl.BlockSpec((toks, rows), lambda i, s: (0, s[k]))

    first, rest = call(
        pack_kernel,
        jnp.stack([column(1 - y_hi, r) for r in range(4)]).astype(jnp.int32),
        (tokens, tokens, tokens, tokens, value_cotangent),
        [block_of(2), block_of(1), block_of(3), block_of(0), whole((toks, feats))],
        (
            jax.ShapeDtypeStruct((toks, rows + feats), BF16),
            jax.ShapeDtypeStruct((toks, 3 * rows), BF16),
        ),
        (whole((toks, rows + feats)), whole((toks, 3 * rows))),
        0,
        4 * toks * (4 * rows + feats),
    )
    first = send(first, across)
    rest = send(after(rest, weight1, left0, right0), across)

    left1, right1 = ring(after(weight1, left0, right0))

    total = after(total, left0, right0, weight1)
    for step in (2, 6):
        got = send(total, flip(0, step, 0, 0))
        total = (total.astype(F32) + got.astype(F32)).astype(BF16)

    def forward(pieces, specs_of):
        n = len(pieces)
        count = sum(len(k) for _, _, k in pieces)

        def kernel(s, g, *refs):
            xs, weights = refs[:n], refs[n : n + count]
            grad, vals, block, sems = refs[-4:]
            total = jnp.zeros((toks, feats), F32)
            cot = g[...]
            at_ref = 0
            copies = []
            for i, (_, _, kinds) in enumerate(pieces):
                w = [ref[...] for ref in weights[at_ref : at_ref + len(kinds)]]
                at_ref += len(kinds)
                w = w[0] if len(w) == 1 else jnp.concatenate(w, axis=0)
                block[i] = lax.dot_general(
                    cot, w, (((1,), (1,)), ((), ())), preferred_element_type=F32
                ).astype(BF16)
                here = pl.ds(pl.multiple_of(s[i] * rows, 128), rows)
                copies.append(pltpu.make_async_copy(block.at[i], grad.at[:, here], sems.at[i]))
                copies[-1].start()
                total += jnp.dot(xs[i][...], w, preferred_element_type=F32)
            vals[...] = total.astype(vals.dtype)
            for copy in copies:
                copy.wait()

        scalars = jnp.stack([column(plane, r) for plane, r, _ in pieces]).astype(jnp.int32)
        operands = [value_cotangent] + [tokens] * n + [k for _, _, kinds in pieces for k in kinds]
        specs = [whole((toks, feats))]
        specs += [pl.BlockSpec((toks, rows), lambda i, s, j=j: (0, s[j])) for j in range(n)]
        specs += specs_of
        return call(
            kernel,
            scalars,
            operands,
            specs,
            (jax.ShapeDtypeStruct(tokens.shape, BF16), jax.ShapeDtypeStruct((toks, feats), F32)),
            (pl.BlockSpec(memory_space=pl.ANY), whole((toks, feats))),
            4 * n * toks * rows * feats,
            2 * n * (2 * toks * rows + rows * feats) + 8 * toks * feats,
            {},
            [pltpu.VMEM((n, toks, rows), BF16), pltpu.SemaphoreType.DMA((n,))],
        )

    blocks = [whole((rows, feats))] * 4
    scal_w = jnp.stack([column(y_hi, r) for r in range(4)]).astype(jnp.int32)
    part = whole((half, feats))

    def block_of_own(k):
        return pl.BlockSpec((toks, rows), lambda i, s: (0, s[k]))

    def first_kernel(s, xa, ga, xg, left, right, up, down):
        total = dot_t(xa[...], ga[...]) + dot_t(xg[:, :rows], xg[:, rows:])
        up[:half] = left[...]
        down[:half] = right[...]
        up[half:] = total[:half].astype(BF16)
        down[half:] = total[half:].astype(BF16)

    up, down = call(
        first_kernel,
        scal_w,
        (tokens, value_cotangent, first, left0, right0),
        [
            block_of_own(2),
            whole((toks, feats)),
            whole((toks, rows + feats)),
            part,
            pl.BlockSpec((half, feats), lambda i, s: (1, 0)),
        ],
        (jax.ShapeDtypeStruct((rows, feats), BF16),) * 2,
        (whole((rows, feats)),) * 2,
        4 * toks * rows * feats,
        2 * toks * (2 * rows + 2 * feats) + 2 * rows * feats,
    )
    up, down, _, _ = lax.optimization_barrier((up, down, left1, right1))
    from_left, from_right = send(up, right_on), send(down, left_on)


    def second_kernel(s, xa1, xa3, xa0, ga, xb, xg, one, three, own):
        g0, g1 = ga[...], xg[:, rows:]
        one[...] = dot_t(xa1[...], g0) + dot_t(xb[:, :rows], g1)
        three[...] = dot_t(xa3[...], g0) + dot_t(xb[:, rows : 2 * rows], g1)
        own[...] = dot_t(xa0[...], g0) + dot_t(xb[:, 2 * rows :], g1)

    one, three, own = call(
        second_kernel,
        scal_w,
        (tokens, tokens, tokens, value_cotangent, rest, first),
        [
            block_of_own(1),
            block_of_own(3),
            block_of_own(0),
            whole((toks, feats)),
            whole((toks, 3 * rows)),
            whole((toks, rows + feats)),
        ],
        (jax.ShapeDtypeStruct((rows, feats), F32),) * 3,
        (whole((rows, feats)),) * 3,
        12 * toks * rows * feats,
        2 * toks * (6 * rows + 2 * feats) + 10 * rows * feats,
    )

    def third_kernel(s, one, three, left, right, up, down, far):
        far[:half] = left[:half]
        far[half:] = right[:half]
        up[:half] = (one[:half] + left[half:].astype(F32)).astype(BF16)
        up[half:] = one[half:].astype(BF16)
        down[:half] = three[:half].astype(BF16)
        down[half:] = (three[half:] + right[half:].astype(F32)).astype(BF16)

    up, down, far1 = call(
        third_kernel,
        scal_w,
        (one, three, from_left, from_right),
        [whole((rows, feats))] * 4,
        (jax.ShapeDtypeStruct((rows, feats), BF16),) * 3,
        (whole((rows, feats)),) * 3,
        2 * rows * feats,
        14 * rows * feats,
    )
    sum_left, sum_right = send(up, right_on), send(down, left_on)
    far1 = send(far1, across)

    total = after(total, rest)
    got = send(total, pair_l)
    total = (total.astype(F32) + got.astype(F32)).astype(BF16)
    got = send(total, pair_z)
    total = lax.select(bit == 0, jnp.concatenate([total, got]), jnp.concatenate([got, total]))
    got = send(total, pair_c)

    def update_kernel(s, a, b, mom, glob, new_mom, new_glob):
        for r, ref in enumerate((a, b)):
            here = pl.ds(pl.multiple_of((s[0] ^ r) * halves, 16), halves)
            average = ref[...].astype(F32) / jnp.float32(32)
            moment = 0.9 * mom[here] + average
            new_mom[here] = moment
            new_glob[here] = glob[here] - 0.7 * (average + 0.9 * moment)

    state = jax.ShapeDtypeStruct((rows, feats), F32)
    new_momentum, new_global = call(
        update_kernel,
        core.astype(jnp.int32)[None],
        (total, got, momentum, global_weight),
        [whole((halves, feats))] * 2 + [whole((rows, feats))] * 2,
        (state, state),
        (whole((rows, feats)),) * 2,
        8 * rows * feats,
        18 * rows * feats,
    )

    full = whole((rows, feats))
    grad, partial_values = forward(
        [
            (1 - y_hi, 0, (weight1,)),
            (1 - y_hi, 3, (left1,)),
            (1 - y_hi, 1, (right1,)),
            (y_hi, 0, (weight,)),
            (y_hi, 3, (left0,)),
            (y_hi, 1, (right0,)),
            (y_hi, 2, (from_left, from_right)),
        ],
        [full] * 6 + [part] * 2,
    )

    def last_kernel(s, g, xr, w, before, own, a, b, old, grad, vals, out):
        w = w[...]
        grad[...] = lax.dot_general(
            g[...], w, (((1,), (1,)), ((), ())), preferred_element_type=F32
        ).astype(BF16)
        vals[...] = (before[...] + jnp.dot(xr[...], w, preferred_element_type=F32)).astype(BF16)
        out[0] = (own[...] + a[...].astype(F32) + b[...].astype(F32)).astype(BF16)

    last_block = pl.BlockSpec((toks, rows), lambda i, s: (0, s[0]))
    token_grad, values, weight_grad = call(
        last_kernel,
        column(1 - y_hi, 2).astype(jnp.int32)[None],
        (value_cotangent, tokens, far1, partial_values, own, sum_left, sum_right, grad),
        [whole((toks, feats)), last_block, full, whole((toks, feats))] + [full] * 3 + [pl.BlockSpec(memory_space=pl.ANY)],
        (
            jax.ShapeDtypeStruct(tokens.shape, BF16),
            jax.ShapeDtypeStruct((toks, feats), BF16),
            jax.ShapeDtypeStruct((1, rows, feats), BF16),
        ),
        (last_block, whole((toks, feats)), whole((1, rows, feats))),
        4 * toks * rows * feats,
        2 * (2 * toks * rows + rows * feats) + 8 * toks * feats + 10 * rows * feats,
        {8: 0},
    )
    return (values, token_grad, weight_grad, new_momentum, new_global)


def solution(mesh):
    in_specs = (
        P(("rep", "fsdp"), None),
        P(("rep", "fsdp"), None),
        P("rep", "fsdp", None),
        P("rep", "fsdp", None),
        P("fsdp", None),
        P("fsdp", None),
    )
    out_specs = (
        P(("rep", "fsdp"), None),
        P(("rep", "fsdp"), None),
        P("rep", "fsdp", None),
        P("fsdp", None),
        P("fsdp", None),
    )
    return jax.shard_map(local, mesh=mesh, in_specs=in_specs, out_specs=out_specs, check_vma=False)
```

time: 258 us -> 92 us (0.36)
  waiting for transfers between devices: 220 us -> 14.6 us
  starting transfers between devices: 0.12 us -> 38 us
  Pallas kernels: 0 us -> 21.4 us
  between operations: 15.5 us -> 0.8 us
  matrix products: 13.5 us -> 0 us
  local copies, waits for them, and re-layouts: 0.02 us -> 9.56 us
    psum x1 -> x0, waiting for transfers between devices: 219 us -> none  [local(): lax.psum(outer_delta[0].astype(jnp.bfloat16), 'rep').astype(jnp.float32)]
    ppermute x0 -> x19, starting transfers between devices: none -> 38 us  [send(): return lax.ppermute(value, AXES, moves)]
    pallas_call x0 -> x7, Pallas kernels: none -> 21.4 us  [call(): pl.pallas_call(kernel, grid_spec=pltpu.PrefetchScalarGridSpec(num_scalar_...]
    ppermute x0 -> x19, waiting for transfers between devices: none -> 14.6 us  [send(): return lax.ppermute(value, AXES, moves)]
    dot_general x3 -> x0, matrix products: 13.5 us -> none  [the longest x1 5.74 us: local(): lax.dot_general(value_cotangent, full_weight, (((1,), (1,)), ((), ())), p...]
    unnamed x6 -> x30, local copies, waits for them, and re-layouts: 0.02 us -> 6.94 us
    sub x1 -> x0, other arithmetic: 3.91 us -> none  [local(): new_global = global_weight - 0.7 * (average + 0.9 * new_momentum)]
  transfers between devices with their start and end apart: 3 -> 19, of which waited for: 1 -> 6; matrix products, arithmetic and copies ran while one was open for 7% -> 11% of each run, Pallas kernels for 0% -> 20%
where the time goes in v2:
time: 92 us; the launch traced here: 91.4 us
  starting transfers between devices  38 us (41%)
  Pallas kernels  21.4 us (23%)
  waiting for transfers between devices  14.6 us (16%)
  local copies, waits for them, and re-layouts  9.56 us (10%)
  other arithmetic  7.09 us (8%)
    ppermute x19, starting transfers between devices, send(): return lax.ppermute(value, AXES, moves)  38 us
    pallas_call x7, Pallas kernels, call(): pl.pallas_call(kernel, grid_spec=pltpu.PrefetchScalarGridSpec(num_scalar_...  21.4 us
    ppermute x19, waiting for transfers between devices, send(): return lax.ppermute(value, AXES, moves)  14.6 us
    unnamed x30, local copies, waits for them, and re-layouts  6.94 us
    select_n x1, other arithmetic, local(): lax.select(bit == 0, jnp.concatenate([total, got]), jnp.concatenate([got,...  1.97 us
    convert_element_type x1, local copies, waits for them, and re-layouts, local(): lax.dynamic_slice(delta, ((1 - core) * halves, 0), (halves, feats))  1.85 us
  transfers between devices with their start and end apart: 19, of which 6 were waited for; matrix products, arithmetic and copies ran while one was open for 11% of the time, Pallas kernels for 20%

profile of v2, /device:TPU:1, one launch (start us, length us, event | category | flops | bytes accessed | tf_op | source)
XLA Modules:
  0.0 91.4 jit_solution(8892681274540731283)
XLA Ops:
  0.6 3.8 %collective-permute-start = (bf16[640,512]{1,0:T(8,128)(2,1)}, bf16[640,512]{1,0:T(8,128)(2,1)}, u32[]{:S(2)}, u32[]{:S(2)}) collective-permute-start(bf16[640,512]{1,0:T(8,128)(2,1)} %bitcast.14), channel_id=1, source_target_pairs={{0,4},{1,5},{2,6},{3,7},{4,0},{5,1},{6,2},{7,3},{8,12},{9,13},{10,... | collective-permute-start | bytes 1966088 | tf_op jit(solution)/shard_map/ppermute | solution.py:39
  4.5 1.2 %collective-permute-start.1 = (bf16[640,512]{1,0:T(8,128)(2,1)}, bf16[640,512]{1,0:T(8,128)(2,1)S(1)}, u32[]{:S(2)}, u32[]{:S(2)}) collective-permute-start(bf16[640,512]{1,0:T(8,128)(2,1)} %bitcast.15), channel_id=1, source_target_pairs={{0,1},{1,2},{2,3},{3,0},{4,5},{5,6},{6,7},{7,4},{8,9},{9,10},{10,1... | collective-permute-start | bytes 1966088 | tf_op jit(solution)/shard_map/ppermute | solution.py:39
  5.7 1.5 %collective-permute-start.2 = (bf16[640,512]{1,0:T(8,128)(2,1)}, bf16[640,512]{1,0:T(8,128)(2,1)}, u32[]{:S(2)}, u32[]{:S(2)}) collective-permute-start(bf16[640,512]{1,0:T(8,128)(2,1)} %bitcast.16), channel_id=1, source_target_pairs={{0,3},{1,0},{2,1},{3,2},{4,7},{5,4},{6,5},{7,6},{8,11},{9,8},{10,9... | collective-permute-start | bytes 1966088 | tf_op jit(solution)/shard_map/ppermute | solution.py:39
  7.1 1.9 %fusion = bf16[320,512]{1,0:T(8,128)(2,1)} fusion(f32[1,640,512]{2,1,0:T(8,128)} %param.9, s32[]{:T(128)S(6)} %select_n.96), kind=kLoop, calls=%fused_computation.2 | loop fusion | bytes 655364 | tf_op jit(solution)/shard_map/convert_element_type | solution.py:96
  9.0 1.5 %collective-permute-start.12 = (bf16[320,512]{1,0:T(8,128)(2,1)}, bf16[320,512]{1,0:T(8,128)(2,1)}, u32[]{:S(2)}, u32[]{:S(2)}) collective-permute-start(bf16[320,512]{1,0:T(8,128)(2,1)} %fusion), channel_id=1, source_target_pairs={{0,8},{1,9},{2,10},{3,11},{4,12},{5,13},{6,14},{7,15},{8,0},{9,1},... | collective-permute-start | bytes 983048 | tf_op jit(solution)/shard_map/ppermute | solution.py:39
  10.6 1.7 %copy-done = bf16[256,5120]{1,0:T(8,128)(2,1)S(1)} copy-done((bf16[256,5120]{1,0:T(8,128)(2,1)S(1)}, bf16[256,5120]{1,0:T(8,128)(2,1)}, u32[]{:S(2)}) %copy-start) | copy-done | bytes 2621464
  13.3 1.5 %shard_map.101 = (bf16[256,1152]{1,0:T(8,128)(2,1)}, bf16[256,1920]{1,0:T(8,128)(2,1)S(1)}) custom-call(s32[4]{0:T(128)S(1)} %pad_add_fusion.1.s, bf16[256,5120]{1,0:T(8,128)(2,1)S(1)} %copy-done, bf16[256,5120]{1,0:T(8,128)(2,1)S(1)} %copy-done, bf16[256,5120]{1,0:T(8,128)(2,1)S(1)} %copy-done, bf16[256,5120]{1,0:T(8,128)(2,1)S(1)} %copy-done, ...), custom_call_target="tpu_custom_call" | custom-call | bytes 3145728 | tf_op jit(solution)/shard_map/pallas_call | solution.py:55
  15.8 1.8 %collective-permute-start.4 = (bf16[256,1152]{1,0:T(8,128)(2,1)}, bf16[256,1152]{1,0:T(8,128)(2,1)}, u32[]{:S(2)}, u32[]{:S(2)}) collective-permute-start(bf16[256,1152]{1,0:T(8,128)(2,1)} %get-tuple-element.30), channel_id=1, source_target_pairs={{0,4},{1,5},{2,6},{3,7},{4,0},{5,1},{6,2},{7,3},{8,12},{9,13},{10,... | collective-permute-start | bytes 1769480 | tf_op jit(solution)/shard_map/ppermute | solution.py:39
  17.6 1.4 %bitcast_add_fusion = f32[320,512]{1,0:T(8,128)S(1)} fusion(bf16[320,512]{1,0:T(8,128)(2,1)} %collective-permute-done.12, f32[1,640,512]{2,1,0:T(8,128)} %param.9, s32[]{:T(128)S(6)} %select_n.95), kind=kLoop, calls=%fused_computation | loop fusion | flops 327680 | bytes 1638404 | tf_op jit(solution)/shard_map/add | solution.py:97
  19.0 2.3 %collective-permute-done.1.left.refs_11_ = bf16[640,512]{1,0:T(8,128)(2,1)S(1)} collective-permute-done((bf16[640,512]{1,0:T(8,128)(2,1)}, bf16[640,512]{1,0:T(8,128)(2,1)S(1)}, u32[]{:S(2)}, u32[]{:S(2)}) %collective-permute-start.1) | collective-permute-done | bytes 655392 | tf_op jit(solution)/shard_map/ppermute | solution.py:39
  22.2 1.8 %collective-permute-start.6 = (bf16[640,512]{1,0:T(8,128)(2,1)}, bf16[640,512]{1,0:T(8,128)(2,1)}, u32[]{:S(2)}, u32[]{:S(2)}) collective-permute-start(bf16[640,512]{1,0:T(8,128)(2,1)} %collective-permute-done.refs_7_), channel_id=1, source_target_pairs={{0,3},{1,0},{2,1},{3,2},{4,7},{5,4},{6,5},{7,6},{8,11},{9,8},{10,9... | collective-permute-start | bytes 1966088 | tf_op jit(solution)/shard_map/ppermute | solution.py:39
  24.6 1.6 %collective-permute-start.13 = (bf16[160,512]{1,0:T(8,128)(2,1)}, bf16[160,512]{1,0:T(8,128)(2,1)}, u32[]{:S(2)}, u32[]{:S(2)}) collective-permute-start(bf16[160,512]{1,0:T(8,128)(2,1)} %dynamic-slice_convert_fusion.1), channel_id=1, source_target_pairs={{0,16},{1,17},{2,18},{3,19},{4,20},{5,21},{6,22},{7,23},{8,24},{9,... | collective-permute-start | bytes 491528 | tf_op jit(solution)/shard_map/ppermute | solution.py:39
  26.9 2.7 %collective-permute-done.13 = bf16[160,512]{1,0:T(8,128)(2,1)} collective-permute-done((bf16[160,512]{1,0:T(8,128)(2,1)}, bf16[160,512]{1,0:T(8,128)(2,1)}, u32[]{:S(2)}, u32[]{:S(2)}) %collective-permute-start.13) | collective-permute-done | bytes 163872 | tf_op jit(solution)/shard_map/ppermute | solution.py:39
  29.6 1.8 %add_convert_fusion.3 = bf16[160,512]{1,0:T(8,128)(2,1)} fusion(bf16[160,512]{1,0:T(8,128)(2,1)} %collective-permute-done.13, f32[320,512]{1,0:T(8,128)} %copy-done.14, s32[]{:T(128)S(6)} %select_n.97), kind=kLoop, calls=%fused_computation.7 | loop fusion | flops 245760 | bytes 655364 | tf_op jit(solution)/shard_map/convert_element_type | solution.py:101
  31.4 3.0 %collective-permute-start.14 = (bf16[160,512]{1,0:T(8,128)(2,1)}, bf16[160,512]{1,0:T(8,128)(2,1)}, u32[]{:S(2)}, u32[]{:S(2)}) collective-permute-start(bf16[160,512]{1,0:T(8,128)(2,1)} %add_convert_fusion.3), channel_id=1, source_target_pairs={{0,32},{1,33},{2,34},{3,35},{4,36},{5,37},{6,38},{7,39},{8,40},{9,... | collective-permute-start | bytes 491528 | tf_op jit(solution)/shard_map/ppermute | solution.py:39
  34.4 2.3 %shard_map.103 = (bf16[640,512]{1,0:T(8,128)(2,1)S(1)}, bf16[640,512]{1,0:T(8,128)(2,1)S(1)}) custom-call(s32[4]{0:T(128)S(1)} %pad_add_fusion.s, bf16[256,5120]{1,0:T(8,128)(2,1)S(1)} %copy-done.1, bf16[256,512]{1,0:T(8,128)(2,1)S(1)} %copy-done.3, bf16[256,1152]{1,0:T(8,128)(2,1)} %collective-permute-done.4.xg, ...), custom_call_target="tpu_custom_call" | custom-call | flops 335544320 | bytes 1835008 | tf_op jit(solution)/shard_map/pallas_call | solution.py:55
  37.2 2.6 %collective-permute-start.8 = (bf16[640,512]{1,0:T(8,128)(2,1)S(1)}, bf16[640,512]{1,0:T(8,128)(2,1)S(1)}, u32[]{:S(2)}, u32[]{:S(2)}) collective-permute-start(bf16[640,512]{1,0:T(8,128)(2,1)S(1)} %get-tuple-element.37), channel_id=1, source_target_pairs={{0,3},{1,0},{2,1},{3,2},{4,7},{5,4},{6,5},{7,6},{8,11},{9,8},{10,9... | collective-permute-start | bytes 1966088 | tf_op jit(solution)/shard_map/ppermute | solution.py:39
  40.9 6.1 %collective-permute-start.15 = (bf16[160,512]{1,0:T(8,128)(2,1)S(1)}, bf16[160,512]{1,0:T(8,128)(2,1)S(1)}, u32[]{:S(2)}, u32[]{:S(2)}) collective-permute-start(bf16[160,512]{1,0:T(8,128)(2,1)S(1)} %add_convert_fusion.2), channel_id=1, source_target_pairs={{0,96},{1,97},{2,98},{3,99},{4,100},{5,101},{6,102},{7,103},{8,104... | collective-permute-start | bytes 491528 | tf_op jit(solution)/shard_map/ppermute | solution.py:39
  47.0 4.0 %collective-permute-done.15 = bf16[160,512]{1,0:T(8,128)(2,1)S(1)} collective-permute-done((bf16[160,512]{1,0:T(8,128)(2,1)S(1)}, bf16[160,512]{1,0:T(8,128)(2,1)S(1)}, u32[]{:S(2)}, u32[]{:S(2)}) %collective-permute-start.15) | collective-permute-done | bytes 163872 | tf_op jit(solution)/shard_map/ppermute | solution.py:39
  51.1 1.8 %collective-permute-done.3.xb = bf16[256,1920]{1,0:T(8,128)(2,1)} collective-permute-done((bf16[256,1920]{1,0:T(8,128)(2,1)}, bf16[256,1920]{1,0:T(8,128)(2,1)}, u32[]{:S(2)}, u32[]{:S(2)}) %collective-permute-start.3) | collective-permute-done | bytes 983072 | tf_op jit(solution)/shard_map/ppermute | solution.py:39
  52.9 1.6 %collective-permute-start.16 = (bf16[160,512]{1,0:T(8,128)(2,1)S(1)}, bf16[160,512]{1,0:T(8,128)(2,1)S(1)}, u32[]{:S(2)}, u32[]{:S(2)}) collective-permute-start(bf16[160,512]{1,0:T(8,128)(2,1)S(1)} %add_convert_fusion.1), channel_id=1, source_target_pairs={{0,128},{1,129},{2,130},{3,131},{4,132},{5,133},{6,134},{7,135},{8... | collective-permute-start | bytes 491528 | tf_op jit(solution)/shard_map/ppermute | solution.py:39
  54.5 3.1 %shard_map.102 = (f32[640,512]{1,0:T(8,128)S(1)}, f32[640,512]{1,0:T(8,128)S(1)}, f32[640,512]{1,0:T(8,128)S(1)}) custom-call(s32[4]{0:T(128)S(1)} %pad_add_fusion.s, bf16[256,5120]{1,0:T(8,128)(2,1)S(1)} %copy-done.1, bf16[256,5120]{1,0:T(8,128)(2,1)S(1)} %copy-done.1, bf16[256,5120]{1,0:T(8,128)(2,1)S(1)} %copy-done.1, bf16[256,512]{1,0:T(8,128)(2,1)S(1)} %copy-done.3, ...), custom_call_target="tpu_custom_call" | custom-call | flops 1006632960 | bytes 5767168 | tf_op jit(solution)/shard_map/pallas_call | solution.py:55
  57.6 2.1 %shard_map.104 = (bf16[640,512]{1,0:T(8,128)(2,1)}, bf16[640,512]{1,0:T(8,128)(2,1)}, bf16[640,512]{1,0:T(8,128)(2,1)}) custom-call(s32[4]{0:T(128)S(1)} %pad_add_fusion.s, f32[640,512]{1,0:T(8,128)S(1)} %get-tuple-element.31.one, f32[640,512]{1,0:T(8,128)S(1)} %get-tuple-element.32.three, bf16[640,512]{1,0:T(8,128)(2,1)S(1)} %collective-permute-done.7.left.refs_13_, ...), custom_call_target="tpu_custom_call" | custom-call | flops 655360 | bytes 4587520 | tf_op jit(solution)/shard_map/pallas_call | solution.py:55
  59.7 2.2 %collective-permute-start.9 = (bf16[640,512]{1,0:T(8,128)(2,1)}, bf16[640,512]{1,0:T(8,128)(2,1)}, u32[]{:S(2)}, u32[]{:S(2)}) collective-permute-start(bf16[640,512]{1,0:T(8,128)(2,1)} %get-tuple-element.38), channel_id=1, source_target_pairs={{0,4},{1,5},{2,6},{3,7},{4,0},{5,1},{6,2},{7,3},{8,12},{9,13},{10,... | collective-permute-start | bytes 1966088 | tf_op jit(solution)/shard_map/ppermute | solution.py:39
  63.2 1.5 %collective-permute-start.11 = (bf16[640,512]{1,0:T(8,128)(2,1)}, bf16[640,512]{1,0:T(8,128)(2,1)}, u32[]{:S(2)}, u32[]{:S(2)}) collective-permute-start(bf16[640,512]{1,0:T(8,128)(2,1)} %get-tuple-element.42), channel_id=1, source_target_pairs={{0,3},{1,0},{2,1},{3,2},{4,7},{5,4},{6,5},{7,6},{8,11},{9,8},{10,9... | collective-permute-start | bytes 1966088 | tf_op jit(solution)/shard_map/ppermute | solution.py:39
  65.3 1.6 %collective-permute-start.17 = (bf16[160,512]{1,0:T(8,128)(2,1)}, bf16[160,512]{1,0:T(8,128)(2,1)}, u32[]{:S(2)}, u32[]{:S(2)}) collective-permute-start(bf16[160,512]{1,0:T(8,128)(2,1)} %add_convert_fusion), channel_id=1, source_target_pairs={{0,16},{1,17},{2,18},{3,19},{4,20},{5,21},{6,22},{7,23},{8,24},{9,... | collective-permute-start | bytes 491528 | tf_op jit(solution)/shard_map/ppermute | solution.py:39
  67.0 3.3 %collective-permute-done.17 = bf16[160,512]{1,0:T(8,128)(2,1)} collective-permute-done((bf16[160,512]{1,0:T(8,128)(2,1)}, bf16[160,512]{1,0:T(8,128)(2,1)}, u32[]{:S(2)}, u32[]{:S(2)}) %collective-permute-start.17) | collective-permute-done | bytes 163872 | tf_op jit(solution)/shard_map/ppermute | solution.py:39
  70.3 2.0 %maximum_select_fusion.a = bf16[320,512]{1,0:T(8,128)(2,1)} fusion(bf16[160,512]{1,0:T(8,128)(2,1)} %collective-permute-done.17, bf16[160,512]{1,0:T(8,128)(2,1)} %add_convert_fusion, pred[]{:T(512)S(6)} %eq.24), kind=kLoop, calls=%fused_computation.3 | loop fusion | flops 1474560 | bytes 655361 | tf_op jit(solution)/shard_map/select_n | solution.py:263
  72.3 3.3 %collective-permute-start.18 = (bf16[320,512]{1,0:T(8,128)(2,1)}, bf16[320,512]{1,0:T(8,128)(2,1)}, u32[]{:S(2)}, u32[]{:S(2)}) collective-permute-start(bf16[320,512]{1,0:T(8,128)(2,1)} %maximum_select_fusion.a), channel_id=1, source_target_pairs={{0,8},{1,9},{2,10},{3,11},{4,12},{5,13},{6,14},{7,15},{8,0},{9,1},... | collective-permute-start | bytes 983048 | tf_op jit(solution)/shard_map/ppermute | solution.py:39
  79.0 6.1 %shard_map.105 = (bf16[256,5120]{1,0:T(8,128)(2,1)}, f32[256,512]{1,0:T(8,128)S(1)}) custom-call(s32[7]{0:T(128)S(1)} %stack.47.s, bf16[256,512]{1,0:T(8,128)(2,1)S(1)} %copy-done.3, bf16[256,5120]{1,0:T(8,128)(2,1)S(1)} %copy-done.1, bf16[256,5120]{1,0:T(8,128)(2,1)S(1)} %copy-done.1, bf16[256,5120]{1,0:T(8,128)(2,1)S(1)} %copy-done.1, ...), custom_call_target="tpu_custom_call" | custom-call | flops 2348810240 | bytes 10223616 | tf_op jit(solution)/shard_map/pallas_call | solution.py:55
  85.1 3.0 %shard_map.107 = (f32[640,512]{1,0:T(8,128)}, f32[640,512]{1,0:T(8,128)}) custom-call(s32[1]{0:T(128)} %bitcast.9.s, bf16[320,512]{1,0:T(8,128)(2,1)} %maximum_select_fusion.a, bf16[320,512]{1,0:T(8,128)(2,1)} %collective-permute-done.18.b, f32[640,512]{1,0:T(8,128)S(1)} %copy-done.10, f32[640,512]{1,0:T(8,128)S(1)} %copy-done.11), custom_call_target="tpu_custom_call" | custom-call | flops 2621440 | bytes 5898240 | tf_op jit(solution)/shard_map/pallas_call | solution.py:55
  88.2 3.3 %shard_map.106 = (bf16[256,5120]{1,0:T(8,128)(2,1)}, bf16[256,512]{1,0:T(8,128)(2,1)}, bf16[1,640,512]{2,1,0:T(8,128)(2,1)}) custom-call(s32[1]{0:T(128)} %bitcast.s, bf16[256,512]{1,0:T(8,128)(2,1)S(1)} %copy-done.3, bf16[256,5120]{1,0:T(8,128)(2,1)S(1)} %copy-done.1, bf16[640,512]{1,0:T(8,128)(2,1)} %collective-permute-done.9.w, ...), custom_call_target="tpu_custom_call", output_to_operand_aliasing={{0}: (8, {})} | custom-call | flops 335544320 | bytes 5636096 | tf_op jit(solution)/shard_map/pallas_call | solution.py:55
  (54 shorter events, 11.2 us)
Async XLA Ops:
  0.6 18.4 %collective-permute-start = (bf16[640,512]{1,0:T(8,128)(2,1)}, bf16[640,512]{1,0:T(8,128)(2,1)}, u32[]{:S(2)}, u32[]{:S(2)}) collective-permute-start(bf16[640,512]{1,0:T(8,128)(2,1)} %bitcast.14), channel_id=1, source_target_pairs={{0,4},{1,5},{2,6},{3,7},{4,0},{5,1},{6,2},{7,3},{8,12},{9,13},{10,... | collective-permute-start | bytes 1966088 | tf_op jit(solution)/shard_map/ppermute | solution.py:39
  4.5 16.8 %collective-permute-start.1 = (bf16[640,512]{1,0:T(8,128)(2,1)}, bf16[640,512]{1,0:T(8,128)(2,1)S(1)}, u32[]{:S(2)}, u32[]{:S(2)}) collective-permute-start(bf16[640,512]{1,0:T(8,128)(2,1)} %bitcast.15), channel_id=1, source_target_pairs={{0,1},{1,2},{2,3},{3,0},{4,5},{5,6},{6,7},{7,4},{8,9},{9,10},{10,1... | collective-permute-start | bytes 1966088 | tf_op jit(solution)/shard_map/ppermute | solution.py:39
  5.7 15.6 %collective-permute-start.2 = (bf16[640,512]{1,0:T(8,128)(2,1)}, bf16[640,512]{1,0:T(8,128)(2,1)}, u32[]{:S(2)}, u32[]{:S(2)}) collective-permute-start(bf16[640,512]{1,0:T(8,128)(2,1)} %bitcast.16), channel_id=1, source_target_pairs={{0,3},{1,0},{2,1},{3,2},{4,7},{5,4},{6,5},{7,6},{8,11},{9,8},{10,9... | collective-permute-start | bytes 1966088 | tf_op jit(solution)/shard_map/ppermute | solution.py:39
  9.0 8.6 %collective-permute-start.12 = (bf16[320,512]{1,0:T(8,128)(2,1)}, bf16[320,512]{1,0:T(8,128)(2,1)}, u32[]{:S(2)}, u32[]{:S(2)}) collective-permute-start(bf16[320,512]{1,0:T(8,128)(2,1)} %fusion), channel_id=1, source_target_pairs={{0,8},{1,9},{2,10},{3,11},{4,12},{5,13},{6,14},{7,15},{8,0},{9,1},... | collective-permute-start | bytes 983048 | tf_op jit(solution)/shard_map/ppermute | solution.py:39
  10.6 1.7 %copy-start = (bf16[256,5120]{1,0:T(8,128)(2,1)S(1)}, bf16[256,5120]{1,0:T(8,128)(2,1)}, u32[]{:S(2)}) copy-start(bf16[256,5120]{1,0:T(8,128)(2,1)} %xr.1) | copy-start | bytes 7864324
  13.3 21.2 %copy-start.3 = (bf16[256,512]{1,0:T(8,128)(2,1)S(1)}, bf16[256,512]{1,0:T(8,128)(2,1)}, u32[]{:S(2)}) copy-start(bf16[256,512]{1,0:T(8,128)(2,1)} %g.3) | copy-start | bytes 786436
  15.8 18.7 %collective-permute-start.4 = (bf16[256,1152]{1,0:T(8,128)(2,1)}, bf16[256,1152]{1,0:T(8,128)(2,1)}, u32[]{:S(2)}, u32[]{:S(2)}) collective-permute-start(bf16[256,1152]{1,0:T(8,128)(2,1)} %get-tuple-element.30), channel_id=1, source_target_pairs={{0,4},{1,5},{2,6},{3,7},{4,0},{5,1},{6,2},{7,3},{8,12},{9,13},{10,... | collective-permute-start | bytes 1769480 | tf_op jit(solution)/shard_map/ppermute | solution.py:39
  17.5 16.9 %copy-start.1 = (bf16[256,5120]{1,0:T(8,128)(2,1)S(1)}, bf16[256,5120]{1,0:T(8,128)(2,1)}, u32[]{:S(2)}) copy-start(bf16[256,5120]{1,0:T(8,128)(2,1)} %xr.1) | copy-start | bytes 7864324
  19.0 5.0 %copy-start.14 = (f32[320,512]{1,0:T(8,128)}, f32[320,512]{1,0:T(8,128)S(1)}, u32[]{:S(2)}) copy-start(f32[320,512]{1,0:T(8,128)S(1)} %bitcast_add_fusion) | copy-start | bytes 1966084
  21.3 15.9 %collective-permute-start.5 = (bf16[640,512]{1,0:T(8,128)(2,1)}, bf16[640,512]{1,0:T(8,128)(2,1)}, u32[]{:S(2)}, u32[]{:S(2)}) collective-permute-start(bf16[640,512]{1,0:T(8,128)(2,1)} %collective-permute-done.refs_7_), channel_id=1, source_target_pairs={{0,1},{1,2},{2,3},{3,0},{4,5},{5,6},{6,7},{7,4},{8,9},{9,10},{10,1... | collective-permute-start | bytes 1966088 | tf_op jit(solution)/shard_map/ppermute | solution.py:39
  22.2 15.0 %collective-permute-start.6 = (bf16[640,512]{1,0:T(8,128)(2,1)}, bf16[640,512]{1,0:T(8,128)(2,1)}, u32[]{:S(2)}, u32[]{:S(2)}) collective-permute-start(bf16[640,512]{1,0:T(8,128)(2,1)} %collective-permute-done.refs_7_), channel_id=1, source_target_pairs={{0,3},{1,0},{2,1},{3,2},{4,7},{5,4},{6,5},{7,6},{8,11},{9,8},{10,9... | collective-permute-start | bytes 1966088 | tf_op jit(solution)/shard_map/ppermute | solution.py:39
  24.6 5.0 %collective-permute-start.13 = (bf16[160,512]{1,0:T(8,128)(2,1)}, bf16[160,512]{1,0:T(8,128)(2,1)}, u32[]{:S(2)}, u32[]{:S(2)}) collective-permute-start(bf16[160,512]{1,0:T(8,128)(2,1)} %dynamic-slice_convert_fusion.1), channel_id=1, source_target_pairs={{0,16},{1,17},{2,18},{3,19},{4,20},{5,21},{6,22},{7,23},{8,24},{9,... | collective-permute-start | bytes 491528 | tf_op jit(solution)/shard_map/ppermute | solution.py:39
  26.3 26.6 %collective-permute-start.3 = (bf16[256,1920]{1,0:T(8,128)(2,1)}, bf16[256,1920]{1,0:T(8,128)(2,1)}, u32[]{:S(2)}, u32[]{:S(2)}) collective-permute-start(bf16[256,1920]{1,0:T(8,128)(2,1)} %copy-done.13), channel_id=1, source_target_pairs={{0,4},{1,5},{2,6},{3,7},{4,0},{5,1},{6,2},{7,3},{8,12},{9,13},{10,... | collective-permute-start | bytes 2949128 | tf_op jit(solution)/shard_map/ppermute | solution.py:39
  31.4 8.5 %collective-permute-start.14 = (bf16[160,512]{1,0:T(8,128)(2,1)}, bf16[160,512]{1,0:T(8,128)(2,1)}, u32[]{:S(2)}, u32[]{:S(2)}) collective-permute-start(bf16[160,512]{1,0:T(8,128)(2,1)} %add_convert_fusion.3), channel_id=1, source_target_pairs={{0,32},{1,33},{2,34},{3,35},{4,36},{5,37},{6,38},{7,39},{8,40},{9,... | collective-permute-start | bytes 491528 | tf_op jit(solution)/shard_map/ppermute | solution.py:39
  37.2 20.4 %collective-permute-start.7 = (bf16[640,512]{1,0:T(8,128)(2,1)S(1)}, bf16[640,512]{1,0:T(8,128)(2,1)S(1)}, u32[]{:S(2)}, u32[]{:S(2)}) collective-permute-start(bf16[640,512]{1,0:T(8,128)(2,1)S(1)} %get-tuple-element.36), channel_id=1, source_target_pairs={{0,1},{1,2},{2,3},{3,0},{4,5},{5,6},{6,7},{7,4},{8,9},{9,10},{10,1... | collective-permute-start | bytes 1966088 | tf_op jit(solution)/shard_map/ppermute | solution.py:39
  37.2 20.4 %collective-permute-start.8 = (bf16[640,512]{1,0:T(8,128)(2,1)S(1)}, bf16[640,512]{1,0:T(8,128)(2,1)S(1)}, u32[]{:S(2)}, u32[]{:S(2)}) collective-permute-start(bf16[640,512]{1,0:T(8,128)(2,1)S(1)} %get-tuple-element.37), channel_id=1, source_target_pairs={{0,3},{1,0},{2,1},{3,2},{4,7},{5,4},{6,5},{7,6},{8,11},{9,8},{10,9... | collective-permute-start | bytes 1966088 | tf_op jit(solution)/shard_map/ppermute | solution.py:39
  40.9 10.1 %collective-permute-start.15 = (bf16[160,512]{1,0:T(8,128)(2,1)S(1)}, bf16[160,512]{1,0:T(8,128)(2,1)S(1)}, u32[]{:S(2)}, u32[]{:S(2)}) collective-permute-start(bf16[160,512]{1,0:T(8,128)(2,1)S(1)} %add_convert_fusion.2), channel_id=1, source_target_pairs={{0,96},{1,97},{2,98},{3,99},{4,100},{5,101},{6,102},{7,103},{8,104... | collective-permute-start | bytes 491528 | tf_op jit(solution)/shard_map/ppermute | solution.py:39
  52.9 11.8 %collective-permute-start.16 = (bf16[160,512]{1,0:T(8,128)(2,1)S(1)}, bf16[160,512]{1,0:T(8,128)(2,1)S(1)}, u32[]{:S(2)}, u32[]{:S(2)}) collective-permute-start(bf16[160,512]{1,0:T(8,128)(2,1)S(1)} %add_convert_fusion.1), channel_id=1, source_target_pairs={{0,128},{1,129},{2,130},{3,131},{4,132},{5,133},{6,134},{7,135},{8... | collective-permute-start | bytes 491528 | tf_op jit(solution)/shard_map/ppermute | solution.py:39
  57.6 2.1 %copy-start.8 = (f32[640,512]{1,0:T(8,128)}, f32[640,512]{1,0:T(8,128)S(1)}, u32[]{:S(2)}) copy-start(f32[640,512]{1,0:T(8,128)S(1)} %get-tuple-element.40.own) | copy-start | bytes 3932164
  57.6 2.1 %copy-start.4 = (bf16[640,512]{1,0:T(8,128)(2,1)}, bf16[640,512]{1,0:T(8,128)(2,1)S(1)}, u32[]{:S(2)}) copy-start(bf16[640,512]{1,0:T(8,128)(2,1)S(1)} %collective-permute-done.7.left.refs_13_) | copy-start | bytes 1966084
  57.6 2.1 %copy-start.6 = (bf16[640,512]{1,0:T(8,128)(2,1)}, bf16[640,512]{1,0:T(8,128)(2,1)S(1)}, u32[]{:S(2)}) copy-start(bf16[640,512]{1,0:T(8,128)(2,1)S(1)} %collective-permute-done.8.right.refs_14_) | copy-start | bytes 1966084
  59.7 28.4 %collective-permute-start.9 = (bf16[640,512]{1,0:T(8,128)(2,1)}, bf16[640,512]{1,0:T(8,128)(2,1)}, u32[]{:S(2)}, u32[]{:S(2)}) collective-permute-start(bf16[640,512]{1,0:T(8,128)(2,1)} %get-tuple-element.38), channel_id=1, source_target_pairs={{0,4},{1,5},{2,6},{3,7},{4,0},{5,1},{6,2},{7,3},{8,12},{9,13},{10,... | collective-permute-start | bytes 1966088 | tf_op jit(solution)/shard_map/ppermute | solution.py:39
  62.0 26.2 %collective-permute-start.10 = (bf16[640,512]{1,0:T(8,128)(2,1)}, bf16[640,512]{1,0:T(8,128)(2,1)}, u32[]{:S(2)}, u32[]{:S(2)}) collective-permute-start(bf16[640,512]{1,0:T(8,128)(2,1)} %get-tuple-element.41), channel_id=1, source_target_pairs={{0,1},{1,2},{2,3},{3,0},{4,5},{5,6},{6,7},{7,4},{8,9},{9,10},{10,1... | collective-permute-start | bytes 1966088 | tf_op jit(solution)/shard_map/ppermute | solution.py:39
  63.2 25.0 %collective-permute-start.11 = (bf16[640,512]{1,0:T(8,128)(2,1)}, bf16[640,512]{1,0:T(8,128)(2,1)}, u32[]{:S(2)}, u32[]{:S(2)}) collective-permute-start(bf16[640,512]{1,0:T(8,128)(2,1)} %get-tuple-element.42), channel_id=1, source_target_pairs={{0,3},{1,0},{2,1},{3,2},{4,7},{5,4},{6,5},{7,6},{8,11},{9,8},{10,9... | collective-permute-start | bytes 1966088 | tf_op jit(solution)/shard_map/ppermute | solution.py:39
  65.3 5.0 %collective-permute-start.17 = (bf16[160,512]{1,0:T(8,128)(2,1)}, bf16[160,512]{1,0:T(8,128)(2,1)}, u32[]{:S(2)}, u32[]{:S(2)}) collective-permute-start(bf16[160,512]{1,0:T(8,128)(2,1)} %add_convert_fusion), channel_id=1, source_target_pairs={{0,16},{1,17},{2,18},{3,19},{4,20},{5,21},{6,22},{7,23},{8,24},{9,... | collective-permute-start | bytes 491528 | tf_op jit(solution)/shard_map/ppermute | solution.py:39
  72.3 12.8 %collective-permute-start.18 = (bf16[320,512]{1,0:T(8,128)(2,1)}, bf16[320,512]{1,0:T(8,128)(2,1)}, u32[]{:S(2)}, u32[]{:S(2)}) collective-permute-start(bf16[320,512]{1,0:T(8,128)(2,1)} %maximum_select_fusion.a), channel_id=1, source_target_pairs={{0,8},{1,9},{2,10},{3,11},{4,12},{5,13},{6,14},{7,15},{8,0},{9,1},... | collective-permute-start | bytes 983048 | tf_op jit(solution)/shard_map/ppermute | solution.py:39
  75.7 1.1 %copy-start.5 = (bf16[640,512]{1,0:T(8,128)(2,1)S(1)}, bf16[640,512]{1,0:T(8,128)(2,1)}, u32[]{:S(2)}) copy-start(bf16[640,512]{1,0:T(8,128)(2,1)} %copy-done.4) | copy-start | bytes 1966084
  76.8 1.1 %copy-start.7 = (bf16[640,512]{1,0:T(8,128)(2,1)S(1)}, bf16[640,512]{1,0:T(8,128)(2,1)}, u32[]{:S(2)}) copy-start(bf16[640,512]{1,0:T(8,128)(2,1)} %copy-done.6) | copy-start | bytes 1966084
  77.9 1.1 %copy-start.12 = (bf16[1,640,512]{2,1,0:T(8,128)(2,1)S(1)}, bf16[1,640,512]{2,1,0:T(8,128)(2,1)}, u32[]{:S(2)}) copy-start(bf16[1,640,512]{2,1,0:T(8,128)(2,1)} %param.8) | copy-start | bytes 1966084
  79.0 6.1 %copy-start.10 = (f32[640,512]{1,0:T(8,128)S(1)}, f32[640,512]{1,0:T(8,128)}, u32[]{:S(2)}) copy-start(f32[640,512]{1,0:T(8,128)} %mom.1) | copy-start | bytes 3932164
  79.0 6.1 %copy-start.11 = (f32[640,512]{1,0:T(8,128)S(1)}, f32[640,512]{1,0:T(8,128)}, u32[]{:S(2)}) copy-start(f32[640,512]{1,0:T(8,128)} %glob.1) | copy-start | bytes 3932164
  85.1 3.0 %copy-start.9 = (f32[640,512]{1,0:T(8,128)S(1)}, f32[640,512]{1,0:T(8,128)}, u32[]{:S(2)}) copy-start(f32[640,512]{1,0:T(8,128)} %copy-done.8) | copy-start | bytes 3932164
  (2 other events, 1.9 us)

commit v3 on v2

--- a/solution.py
+++ b/solution.py
@@ -51,7 +51,7 @@
     return pl.BlockSpec(shape, lambda i, s: (0,) * len(shape))
 
 
-def call(kernel, scalars, operands, specs, outs, out_specs, flops, moved, aliases={}, scratch=()):
+def call(kernel, scalars, operands, specs, outs, out_specs, flops, moved, aliases={}, scratch=(), vmem=32):
     return pl.pallas_call(
         kernel,
         grid_spec=pltpu.PrefetchScalarGridSpec(
@@ -60,7 +60,7 @@
         out_shape=outs,
         input_output_aliases=aliases,
         cost_estimate=pl.CostEstimate(flops=flops, bytes_accessed=moved, transcendentals=0),
-        compiler_params=pltpu.CompilerParams(vmem_limit_bytes=32 * 2**20),
+        compiler_params=pltpu.CompilerParams(vmem_limit_bytes=vmem * 2**20),
     )(scalars, *operands)
 
 
@@ -174,7 +174,8 @@
             4 * n * toks * rows * feats,
             2 * n * (2 * toks * rows + rows * feats) + 8 * toks * feats,
             {},
-            [pltpu.VMEM((n, toks, rows), BF16), pltpu.SemaphoreType.DMA((n,))],
+            vmem=60,
+            scratch=[pltpu.VMEM((n, toks, rows), BF16), pltpu.SemaphoreType.DMA((n,))],
         )
 
     blocks = [whole((rows, feats))] * 4

time: 92 us -> 90.7 us (0.986)
  Pallas kernels: 21.4 us -> 24 us
  other arithmetic: 7.09 us -> 5.3 us
  local copies, waits for them, and re-layouts: 9.56 us -> 7.86 us
    pallas_call x7, Pallas kernels: 21.4 us -> 24 us  [call(): pl.pallas_call(kernel, grid_spec=pltpu.PrefetchScalarGridSpec(num_scalar_...]
    unnamed x30 -> x32, local copies, waits for them, and re-layouts: 6.94 us -> 4.72 us
    select_n x1, other arithmetic: 1.97 us -> 0.85 us  [local(): lax.select(bit == 0, jnp.concatenate([total, got]), jnp.concatenate([got,...]
  transfers between devices with their start and end apart: 19 -> 19, of which waited for: 6 -> 6; matrix products, arithmetic and copies ran while one was open for 11% -> 9% of each run, Pallas kernels for 20% -> 23%
where the time goes in v3:
time: 90.7 us; the launch traced here: 90.4 us
  starting transfers between devices  38 us (42%)
  Pallas kernels  24 us (26%)
  waiting for transfers between devices  14.3 us (16%)
  local copies, waits for them, and re-layouts  7.86 us (9%)
  other arithmetic  5.3 us (6%)
    ppermute x19, starting transfers between devices, send(): return lax.ppermute(value, AXES, moves)  38 us
    pallas_call x7, Pallas kernels, call(): pl.pallas_call(kernel, grid_spec=pltpu.PrefetchScalarGridSpec(num_scalar_...  24 us
    ppermute x19, waiting for transfers between devices, send(): return lax.ppermute(value, AXES, moves)  14.3 us
    unnamed x32, local copies, waits for them, and re-layouts  4.72 us
    convert_element_type x1, local copies, waits for them, and re-layouts, local(): lax.dynamic_slice(delta, ((1 - core) * halves, 0), (halves, feats))  1.85 us
  transfers between devices with their start and end apart: 19, of which 6 were waited for; matrix products, arithmetic and copies ran while one was open for 9% of the time, Pallas kernels for 23%

profile of v3, /device:TPU:1, one launch (start us, length us, event | category | flops | bytes accessed | tf_op | source)
XLA Modules:
  0.0 90.4 jit_solution(13171278242905339811)
XLA Ops:
  0.6 3.8 %collective-permute-start = (bf16[640,512]{1,0:T(8,128)(2,1)}, bf16[640,512]{1,0:T(8,128)(2,1)}, u32[]{:S(2)}, u32[]{:S(2)}) collective-permute-start(bf16[640,512]{1,0:T(8,128)(2,1)} %bitcast.14), channel_id=1, source_target_pairs={{0,4},{1,5},{2,6},{3,7},{4,0},{5,1},{6,2},{7,3},{8,12},{9,13},{10,... | collective-permute-start | bytes 1966088 | tf_op jit(solution)/shard_map/ppermute | solution.py:39
  4.5 1.2 %collective-permute-start.1 = (bf16[640,512]{1,0:T(8,128)(2,1)}, bf16[640,512]{1,0:T(8,128)(2,1)S(1)}, u32[]{:S(2)}, u32[]{:S(2)}) collective-permute-start(bf16[640,512]{1,0:T(8,128)(2,1)} %bitcast.15), channel_id=1, source_target_pairs={{0,1},{1,2},{2,3},{3,0},{4,5},{5,6},{6,7},{7,4},{8,9},{9,10},{10,1... | collective-permute-start | bytes 1966088 | tf_op jit(solution)/shard_map/ppermute | solution.py:39
  5.7 1.5 %collective-permute-start.2 = (bf16[640,512]{1,0:T(8,128)(2,1)}, bf16[640,512]{1,0:T(8,128)(2,1)}, u32[]{:S(2)}, u32[]{:S(2)}) collective-permute-start(bf16[640,512]{1,0:T(8,128)(2,1)} %bitcast.16), channel_id=1, source_target_pairs={{0,3},{1,0},{2,1},{3,2},{4,7},{5,4},{6,5},{7,6},{8,11},{9,8},{10,9... | collective-permute-start | bytes 1966088 | tf_op jit(solution)/shard_map/ppermute | solution.py:39
  7.1 1.9 %fusion = bf16[320,512]{1,0:T(8,128)(2,1)} fusion(f32[1,640,512]{2,1,0:T(8,128)} %param.9, s32[]{:T(128)S(6)} %select_n.96), kind=kLoop, calls=%fused_computation.2 | loop fusion | bytes 655364 | tf_op jit(solution)/shard_map/convert_element_type | solution.py:96
  9.0 1.5 %collective-permute-start.12 = (bf16[320,512]{1,0:T(8,128)(2,1)}, bf16[320,512]{1,0:T(8,128)(2,1)}, u32[]{:S(2)}, u32[]{:S(2)}) collective-permute-start(bf16[320,512]{1,0:T(8,128)(2,1)} %fusion), channel_id=1, source_target_pairs={{0,8},{1,9},{2,10},{3,11},{4,12},{5,13},{6,14},{7,15},{8,0},{9,1},... | collective-permute-start | bytes 983048 | tf_op jit(solution)/shard_map/ppermute | solution.py:39
  10.6 1.7 %copy-done = bf16[256,5120]{1,0:T(8,128)(2,1)S(1)} copy-done((bf16[256,5120]{1,0:T(8,128)(2,1)S(1)}, bf16[256,5120]{1,0:T(8,128)(2,1)}, u32[]{:S(2)}) %copy-start) | copy-done | bytes 2621464
  13.3 1.5 %shard_map.101 = (bf16[256,1152]{1,0:T(8,128)(2,1)}, bf16[256,1920]{1,0:T(8,128)(2,1)S(1)}) custom-call(s32[4]{0:T(128)S(1)} %pad_add_fusion.1.s, bf16[256,5120]{1,0:T(8,128)(2,1)S(1)} %copy-done, bf16[256,5120]{1,0:T(8,128)(2,1)S(1)} %copy-done, bf16[256,5120]{1,0:T(8,128)(2,1)S(1)} %copy-done, bf16[256,5120]{1,0:T(8,128)(2,1)S(1)} %copy-done, ...), custom_call_target="tpu_custom_call" | custom-call | bytes 3145728 | tf_op jit(solution)/shard_map/pallas_call | solution.py:55
  15.8 1.8 %collective-permute-start.4 = (bf16[256,1152]{1,0:T(8,128)(2,1)}, bf16[256,1152]{1,0:T(8,128)(2,1)}, u32[]{:S(2)}, u32[]{:S(2)}) collective-permute-start(bf16[256,1152]{1,0:T(8,128)(2,1)} %get-tuple-element.30), channel_id=1, source_target_pairs={{0,4},{1,5},{2,6},{3,7},{4,0},{5,1},{6,2},{7,3},{8,12},{9,13},{10,... | collective-permute-start | bytes 1769480 | tf_op jit(solution)/shard_map/ppermute | solution.py:39
  17.6 1.4 %bitcast_add_fusion = f32[320,512]{1,0:T(8,128)S(1)} fusion(bf16[320,512]{1,0:T(8,128)(2,1)} %collective-permute-done.12, f32[1,640,512]{2,1,0:T(8,128)} %param.9, s32[]{:T(128)S(6)} %select_n.95), kind=kLoop, calls=%fused_computation | loop fusion | flops 327680 | bytes 1638404 | tf_op jit(solution)/shard_map/add | solution.py:97
  19.0 2.3 %collective-permute-done.1.left.refs_11_ = bf16[640,512]{1,0:T(8,128)(2,1)S(1)} collective-permute-done((bf16[640,512]{1,0:T(8,128)(2,1)}, bf16[640,512]{1,0:T(8,128)(2,1)S(1)}, u32[]{:S(2)}, u32[]{:S(2)}) %collective-permute-start.1) | collective-permute-done | bytes 655392 | tf_op jit(solution)/shard_map/ppermute | solution.py:39
  22.2 1.8 %collective-permute-start.6 = (bf16[640,512]{1,0:T(8,128)(2,1)}, bf16[640,512]{1,0:T(8,128)(2,1)}, u32[]{:S(2)}, u32[]{:S(2)}) collective-permute-start(bf16[640,512]{1,0:T(8,128)(2,1)} %collective-permute-done.refs_7_), channel_id=1, source_target_pairs={{0,3},{1,0},{2,1},{3,2},{4,7},{5,4},{6,5},{7,6},{8,11},{9,8},{10,9... | collective-permute-start | bytes 1966088 | tf_op jit(solution)/shard_map/ppermute | solution.py:39
  24.6 1.6 %collective-permute-start.13 = (bf16[160,512]{1,0:T(8,128)(2,1)}, bf16[160,512]{1,0:T(8,128)(2,1)}, u32[]{:S(2)}, u32[]{:S(2)}) collective-permute-start(bf16[160,512]{1,0:T(8,128)(2,1)} %dynamic-slice_convert_fusion.1), channel_id=1, source_target_pairs={{0,16},{1,17},{2,18},{3,19},{4,20},{5,21},{6,22},{7,23},{8,24},{9,... | collective-permute-start | bytes 491528 | tf_op jit(solution)/shard_map/ppermute | solution.py:39
  27.0 2.6 %collective-permute-done.13 = bf16[160,512]{1,0:T(8,128)(2,1)} collective-permute-done((bf16[160,512]{1,0:T(8,128)(2,1)}, bf16[160,512]{1,0:T(8,128)(2,1)}, u32[]{:S(2)}, u32[]{:S(2)}) %collective-permute-start.13) | collective-permute-done | bytes 163872 | tf_op jit(solution)/shard_map/ppermute | solution.py:39
  29.6 1.8 %add_convert_fusion.3 = bf16[160,512]{1,0:T(8,128)(2,1)} fusion(bf16[160,512]{1,0:T(8,128)(2,1)} %collective-permute-done.13, f32[320,512]{1,0:T(8,128)} %copy-done.15, s32[]{:T(128)S(6)} %select_n.97), kind=kLoop, calls=%fused_computation.7 | loop fusion | flops 245760 | bytes 655364 | tf_op jit(solution)/shard_map/convert_element_type | solution.py:101
  31.4 3.0 %collective-permute-start.14 = (bf16[160,512]{1,0:T(8,128)(2,1)}, bf16[160,512]{1,0:T(8,128)(2,1)}, u32[]{:S(2)}, u32[]{:S(2)}) collective-permute-start(bf16[160,512]{1,0:T(8,128)(2,1)} %add_convert_fusion.3), channel_id=1, source_target_pairs={{0,32},{1,33},{2,34},{3,35},{4,36},{5,37},{6,38},{7,39},{8,40},{9,... | collective-permute-start | bytes 491528 | tf_op jit(solution)/shard_map/ppermute | solution.py:39
  34.4 2.3 %shard_map.103 = (bf16[640,512]{1,0:T(8,128)(2,1)S(1)}, bf16[640,512]{1,0:T(8,128)(2,1)S(1)}) custom-call(s32[4]{0:T(128)S(1)} %pad_add_fusion.s, bf16[256,5120]{1,0:T(8,128)(2,1)S(1)} %copy-done.1, bf16[256,512]{1,0:T(8,128)(2,1)S(1)} %copy-done.4, bf16[256,1152]{1,0:T(8,128)(2,1)} %collective-permute-done.4.xg, ...), custom_call_target="tpu_custom_call" | custom-call | flops 335544320 | bytes 1835008 | tf_op jit(solution)/shard_map/pallas_call | solution.py:55
  37.2 2.6 %collective-permute-start.8 = (bf16[640,512]{1,0:T(8,128)(2,1)S(1)}, bf16[640,512]{1,0:T(8,128)(2,1)S(1)}, u32[]{:S(2)}, u32[]{:S(2)}) collective-permute-start(bf16[640,512]{1,0:T(8,128)(2,1)S(1)} %get-tuple-element.37), channel_id=1, source_target_pairs={{0,3},{1,0},{2,1},{3,2},{4,7},{5,4},{6,5},{7,6},{8,11},{9,8},{10,9... | collective-permute-start | bytes 1966088 | tf_op jit(solution)/shard_map/ppermute | solution.py:39
  40.9 6.1 %collective-permute-start.15 = (bf16[160,512]{1,0:T(8,128)(2,1)S(1)}, bf16[160,512]{1,0:T(8,128)(2,1)S(1)}, u32[]{:S(2)}, u32[]{:S(2)}) collective-permute-start(bf16[160,512]{1,0:T(8,128)(2,1)S(1)} %add_convert_fusion.2), channel_id=1, source_target_pairs={{0,96},{1,97},{2,98},{3,99},{4,100},{5,101},{6,102},{7,103},{8,104... | collective-permute-start | bytes 491528 | tf_op jit(solution)/shard_map/ppermute | solution.py:39
  47.0 4.0 %collective-permute-done.15 = bf16[160,512]{1,0:T(8,128)(2,1)S(1)} collective-permute-done((bf16[160,512]{1,0:T(8,128)(2,1)S(1)}, bf16[160,512]{1,0:T(8,128)(2,1)S(1)}, u32[]{:S(2)}, u32[]{:S(2)}) %collective-permute-start.15) | collective-permute-done | bytes 163872 | tf_op jit(solution)/shard_map/ppermute | solution.py:39
  51.1 1.8 %collective-permute-done.3.xb = bf16[256,1920]{1,0:T(8,128)(2,1)} collective-permute-done((bf16[256,1920]{1,0:T(8,128)(2,1)}, bf16[256,1920]{1,0:T(8,128)(2,1)}, u32[]{:S(2)}, u32[]{:S(2)}) %collective-permute-start.3) | collective-permute-done | bytes 983072 | tf_op jit(solution)/shard_map/ppermute | solution.py:39
  52.9 1.6 %collective-permute-start.16 = (bf16[160,512]{1,0:T(8,128)(2,1)S(1)}, bf16[160,512]{1,0:T(8,128)(2,1)S(1)}, u32[]{:S(2)}, u32[]{:S(2)}) collective-permute-start(bf16[160,512]{1,0:T(8,128)(2,1)S(1)} %add_convert_fusion.1), channel_id=1, source_target_pairs={{0,128},{1,129},{2,130},{3,131},{4,132},{5,133},{6,134},{7,135},{8... | collective-permute-start | bytes 491528 | tf_op jit(solution)/shard_map/ppermute | solution.py:39
  54.5 3.1 %shard_map.102 = (f32[640,512]{1,0:T(8,128)S(1)}, f32[640,512]{1,0:T(8,128)S(1)}, f32[640,512]{1,0:T(8,128)S(1)}) custom-call(s32[4]{0:T(128)S(1)} %pad_add_fusion.s, bf16[256,5120]{1,0:T(8,128)(2,1)S(1)} %copy-done.1, bf16[256,5120]{1,0:T(8,128)(2,1)S(1)} %copy-done.1, bf16[256,5120]{1,0:T(8,128)(2,1)S(1)} %copy-done.1, bf16[256,512]{1,0:T(8,128)(2,1)S(1)} %copy-done.4, ...), custom_call_target="tpu_custom_call" | custom-call | flops 1006632960 | bytes 5767168 | tf_op jit(solution)/shard_map/pallas_call | solution.py:55
  57.6 2.1 %shard_map.104 = (bf16[640,512]{1,0:T(8,128)(2,1)}, bf16[640,512]{1,0:T(8,128)(2,1)}, bf16[640,512]{1,0:T(8,128)(2,1)}) custom-call(s32[4]{0:T(128)S(1)} %pad_add_fusion.s, f32[640,512]{1,0:T(8,128)S(1)} %get-tuple-element.31.one, f32[640,512]{1,0:T(8,128)S(1)} %get-tuple-element.32.three, bf16[640,512]{1,0:T(8,128)(2,1)S(1)} %collective-permute-done.7.left.refs_13_, ...), custom_call_target="tpu_custom_call" | custom-call | flops 655360 | bytes 4587520 | tf_op jit(solution)/shard_map/pallas_call | solution.py:55
  59.7 2.2 %collective-permute-start.9 = (bf16[640,512]{1,0:T(8,128)(2,1)}, bf16[640,512]{1,0:T(8,128)(2,1)}, u32[]{:S(2)}, u32[]{:S(2)}) collective-permute-start(bf16[640,512]{1,0:T(8,128)(2,1)} %get-tuple-element.38), channel_id=1, source_target_pairs={{0,4},{1,5},{2,6},{3,7},{4,0},{5,1},{6,2},{7,3},{8,12},{9,13},{10,... | collective-permute-start | bytes 1966088 | tf_op jit(solution)/shard_map/ppermute | solution.py:39
  62.0 1.2 %collective-permute-start.10 = (bf16[640,512]{1,0:T(8,128)(2,1)}, bf16[640,512]{1,0:T(8,128)(2,1)}, u32[]{:S(2)}, u32[]{:S(2)}) collective-permute-start(bf16[640,512]{1,0:T(8,128)(2,1)} %get-tuple-element.41), channel_id=1, source_target_pairs={{0,1},{1,2},{2,3},{3,0},{4,5},{5,6},{6,7},{7,4},{8,9},{9,10},{10,1... | collective-permute-start | bytes 1966088 | tf_op jit(solution)/shard_map/ppermute | solution.py:39
  63.2 1.5 %collective-permute-start.11 = (bf16[640,512]{1,0:T(8,128)(2,1)}, bf16[640,512]{1,0:T(8,128)(2,1)}, u32[]{:S(2)}, u32[]{:S(2)}) collective-permute-start(bf16[640,512]{1,0:T(8,128)(2,1)} %get-tuple-element.42), channel_id=1, source_target_pairs={{0,3},{1,0},{2,1},{3,2},{4,7},{5,4},{6,5},{7,6},{8,11},{9,8},{10,9... | collective-permute-start | bytes 1966088 | tf_op jit(solution)/shard_map/ppermute | solution.py:39
  64.7 1.7 %collective-permute-start.17 = (bf16[160,512]{1,0:T(8,128)(2,1)S(1)}, bf16[160,512]{1,0:T(8,128)(2,1)S(1)}, u32[]{:S(2)}, u32[]{:S(2)}) collective-permute-start(bf16[160,512]{1,0:T(8,128)(2,1)S(1)} %add_convert_fusion), channel_id=1, source_target_pairs={{0,16},{1,17},{2,18},{3,19},{4,20},{5,21},{6,22},{7,23},{8,24},{9,... | collective-permute-start | bytes 491528 | tf_op jit(solution)/shard_map/ppermute | solution.py:39
  66.4 3.1 %collective-permute-done.17 = bf16[160,512]{1,0:T(8,128)(2,1)S(1)} collective-permute-done((bf16[160,512]{1,0:T(8,128)(2,1)S(1)}, bf16[160,512]{1,0:T(8,128)(2,1)S(1)}, u32[]{:S(2)}, u32[]{:S(2)}) %collective-permute-start.17) | collective-permute-done | bytes 163872 | tf_op jit(solution)/shard_map/ppermute | solution.py:39
  70.4 3.2 %collective-permute-start.18 = (bf16[320,512]{1,0:T(8,128)(2,1)}, bf16[320,512]{1,0:T(8,128)(2,1)}, u32[]{:S(2)}, u32[]{:S(2)}) collective-permute-start(bf16[320,512]{1,0:T(8,128)(2,1)} %maximum_select_fusion.a), channel_id=1, source_target_pairs={{0,8},{1,9},{2,10},{3,11},{4,12},{5,13},{6,14},{7,15},{8,0},{9,1},... | collective-permute-start | bytes 983048 | tf_op jit(solution)/shard_map/ppermute | solution.py:39
  74.2 8.7 %shard_map.105 = (bf16[256,5120]{1,0:T(8,128)(2,1)}, f32[256,512]{1,0:T(8,128)}) custom-call(s32[7]{0:T(128)} %stack.47.s, bf16[256,512]{1,0:T(8,128)(2,1)} %g.3, bf16[256,5120]{1,0:T(8,128)(2,1)} %xr.1, bf16[256,5120]{1,0:T(8,128)(2,1)} %xr.1, bf16[256,5120]{1,0:T(8,128)(2,1)} %xr.1, bf16[256,5120]{1,0:T(8,128)(2,1)} %xr.1, bf16[256,5120]{1,0:T(8,128)(2,1)} %xr.1, ...), custom_call_target="tpu_custom_call" | custom-call | flops 2348810240 | bytes 10223616 | tf_op jit(solution)/shard_map/pallas_call | solution.py:55
  82.9 3.1 %shard_map.107 = (f32[640,512]{1,0:T(8,128)}, f32[640,512]{1,0:T(8,128)}) custom-call(s32[1]{0:T(128)} %bitcast.9.s, bf16[320,512]{1,0:T(8,128)(2,1)} %maximum_select_fusion.a, bf16[320,512]{1,0:T(8,128)(2,1)} %collective-permute-done.18.b, f32[640,512]{1,0:T(8,128)S(1)} %copy-done.11, f32[640,512]{1,0:T(8,128)S(1)} %copy-done.12), custom_call_target="tpu_custom_call" | custom-call | flops 2621440 | bytes 5898240 | tf_op jit(solution)/shard_map/pallas_call | solution.py:55
  87.1 3.3 %shard_map.106 = (bf16[256,5120]{1,0:T(8,128)(2,1)}, bf16[256,512]{1,0:T(8,128)(2,1)}, bf16[1,640,512]{2,1,0:T(8,128)(2,1)}) custom-call(s32[1]{0:T(128)} %bitcast.s, bf16[256,512]{1,0:T(8,128)(2,1)S(1)} %copy-done.5, bf16[256,5120]{1,0:T(8,128)(2,1)S(1)} %copy-done.2, bf16[640,512]{1,0:T(8,128)(2,1)} %collective-permute-done.9.w, ...), custom_call_target="tpu_custom_call", output_to_operand_aliasing={{0}: (8, {})} | custom-call | flops 335544320 | bytes 5636096 | tf_op jit(solution)/shard_map/pallas_call | solution.py:55
  (56 shorter events, 8.5 us)
Async XLA Ops:
  0.6 18.4 %collective-permute-start = (bf16[640,512]{1,0:T(8,128)(2,1)}, bf16[640,512]{1,0:T(8,128)(2,1)}, u32[]{:S(2)}, u32[]{:S(2)}) collective-permute-start(bf16[640,512]{1,0:T(8,128)(2,1)} %bitcast.14), channel_id=1, source_target_pairs={{0,4},{1,5},{2,6},{3,7},{4,0},{5,1},{6,2},{7,3},{8,12},{9,13},{10,... | collective-permute-start | bytes 1966088 | tf_op jit(solution)/shard_map/ppermute | solution.py:39
  4.5 16.8 %collective-permute-start.1 = (bf16[640,512]{1,0:T(8,128)(2,1)}, bf16[640,512]{1,0:T(8,128)(2,1)S(1)}, u32[]{:S(2)}, u32[]{:S(2)}) collective-permute-start(bf16[640,512]{1,0:T(8,128)(2,1)} %bitcast.15), channel_id=1, source_target_pairs={{0,1},{1,2},{2,3},{3,0},{4,5},{5,6},{6,7},{7,4},{8,9},{9,10},{10,1... | collective-permute-start | bytes 1966088 | tf_op jit(solution)/shard_map/ppermute | solution.py:39
  5.7 15.6 %collective-permute-start.2 = (bf16[640,512]{1,0:T(8,128)(2,1)}, bf16[640,512]{1,0:T(8,128)(2,1)}, u32[]{:S(2)}, u32[]{:S(2)}) collective-permute-start(bf16[640,512]{1,0:T(8,128)(2,1)} %bitcast.16), channel_id=1, source_target_pairs={{0,3},{1,0},{2,1},{3,2},{4,7},{5,4},{6,5},{7,6},{8,11},{9,8},{10,9... | collective-permute-start | bytes 1966088 | tf_op jit(solution)/shard_map/ppermute | solution.py:39
  9.0 8.6 %collective-permute-start.12 = (bf16[320,512]{1,0:T(8,128)(2,1)}, bf16[320,512]{1,0:T(8,128)(2,1)}, u32[]{:S(2)}, u32[]{:S(2)}) collective-permute-start(bf16[320,512]{1,0:T(8,128)(2,1)} %fusion), channel_id=1, source_target_pairs={{0,8},{1,9},{2,10},{3,11},{4,12},{5,13},{6,14},{7,15},{8,0},{9,1},... | collective-permute-start | bytes 983048 | tf_op jit(solution)/shard_map/ppermute | solution.py:39
  10.6 1.7 %copy-start = (bf16[256,5120]{1,0:T(8,128)(2,1)S(1)}, bf16[256,5120]{1,0:T(8,128)(2,1)}, u32[]{:S(2)}) copy-start(bf16[256,5120]{1,0:T(8,128)(2,1)} %xr.1) | copy-start | bytes 7864324
  13.3 21.2 %copy-start.4 = (bf16[256,512]{1,0:T(8,128)(2,1)S(1)}, bf16[256,512]{1,0:T(8,128)(2,1)}, u32[]{:S(2)}) copy-start(bf16[256,512]{1,0:T(8,128)(2,1)} %g.3) | copy-start | bytes 786436
  15.8 18.7 %collective-permute-start.4 = (bf16[256,1152]{1,0:T(8,128)(2,1)}, bf16[256,1152]{1,0:T(8,128)(2,1)}, u32[]{:S(2)}, u32[]{:S(2)}) collective-permute-start(bf16[256,1152]{1,0:T(8,128)(2,1)} %get-tuple-element.30), channel_id=1, source_target_pairs={{0,4},{1,5},{2,6},{3,7},{4,0},{5,1},{6,2},{7,3},{8,12},{9,13},{10,... | collective-permute-start | bytes 1769480 | tf_op jit(solution)/shard_map/ppermute | solution.py:39
  17.5 16.9 %copy-start.1 = (bf16[256,5120]{1,0:T(8,128)(2,1)S(1)}, bf16[256,5120]{1,0:T(8,128)(2,1)}, u32[]{:S(2)}) copy-start(bf16[256,5120]{1,0:T(8,128)(2,1)} %xr.1) | copy-start | bytes 7864324
  19.0 5.0 %copy-start.15 = (f32[320,512]{1,0:T(8,128)}, f32[320,512]{1,0:T(8,128)S(1)}, u32[]{:S(2)}) copy-start(f32[320,512]{1,0:T(8,128)S(1)} %bitcast_add_fusion) | copy-start | bytes 1966084
  21.3 15.4 %copy-start.6 = (bf16[640,512]{1,0:T(8,128)(2,1)}, bf16[640,512]{1,0:T(8,128)(2,1)S(1)}, u32[]{:S(2)}) copy-start(bf16[640,512]{1,0:T(8,128)(2,1)S(1)} %collective-permute-done.1.left.refs_11_) | copy-start | bytes 1966084
  21.3 15.9 %collective-permute-start.5 = (bf16[640,512]{1,0:T(8,128)(2,1)}, bf16[640,512]{1,0:T(8,128)(2,1)}, u32[]{:S(2)}, u32[]{:S(2)}) collective-permute-start(bf16[640,512]{1,0:T(8,128)(2,1)} %collective-permute-done.refs_7_), channel_id=1, source_target_pairs={{0,1},{1,2},{2,3},{3,0},{4,5},{5,6},{6,7},{7,4},{8,9},{9,10},{10,1... | collective-permute-start | bytes 1966088 | tf_op jit(solution)/shard_map/ppermute | solution.py:39
  22.2 15.0 %collective-permute-start.6 = (bf16[640,512]{1,0:T(8,128)(2,1)}, bf16[640,512]{1,0:T(8,128)(2,1)}, u32[]{:S(2)}, u32[]{:S(2)}) collective-permute-start(bf16[640,512]{1,0:T(8,128)(2,1)} %collective-permute-done.refs_7_), channel_id=1, source_target_pairs={{0,3},{1,0},{2,1},{3,2},{4,7},{5,4},{6,5},{7,6},{8,11},{9,8},{10,9... | collective-permute-start | bytes 1966088 | tf_op jit(solution)/shard_map/ppermute | solution.py:39
  24.6 5.0 %collective-permute-start.13 = (bf16[160,512]{1,0:T(8,128)(2,1)}, bf16[160,512]{1,0:T(8,128)(2,1)}, u32[]{:S(2)}, u32[]{:S(2)}) collective-permute-start(bf16[160,512]{1,0:T(8,128)(2,1)} %dynamic-slice_convert_fusion.1), channel_id=1, source_target_pairs={{0,16},{1,17},{2,18},{3,19},{4,20},{5,21},{6,22},{7,23},{8,24},{9,... | collective-permute-start | bytes 491528 | tf_op jit(solution)/shard_map/ppermute | solution.py:39
  26.3 26.6 %collective-permute-start.3 = (bf16[256,1920]{1,0:T(8,128)(2,1)}, bf16[256,1920]{1,0:T(8,128)(2,1)}, u32[]{:S(2)}, u32[]{:S(2)}) collective-permute-start(bf16[256,1920]{1,0:T(8,128)(2,1)} %copy-done.14), channel_id=1, source_target_pairs={{0,4},{1,5},{2,6},{3,7},{4,0},{5,1},{6,2},{7,3},{8,12},{9,13},{10,... | collective-permute-start | bytes 2949128 | tf_op jit(solution)/shard_map/ppermute | solution.py:39
  31.4 8.5 %collective-permute-start.14 = (bf16[160,512]{1,0:T(8,128)(2,1)}, bf16[160,512]{1,0:T(8,128)(2,1)}, u32[]{:S(2)}, u32[]{:S(2)}) collective-permute-start(bf16[160,512]{1,0:T(8,128)(2,1)} %add_convert_fusion.3), channel_id=1, source_target_pairs={{0,32},{1,33},{2,34},{3,35},{4,36},{5,37},{6,38},{7,39},{8,40},{9,... | collective-permute-start | bytes 491528 | tf_op jit(solution)/shard_map/ppermute | solution.py:39
  37.2 20.4 %collective-permute-start.7 = (bf16[640,512]{1,0:T(8,128)(2,1)S(1)}, bf16[640,512]{1,0:T(8,128)(2,1)S(1)}, u32[]{:S(2)}, u32[]{:S(2)}) collective-permute-start(bf16[640,512]{1,0:T(8,128)(2,1)S(1)} %get-tuple-element.36), channel_id=1, source_target_pairs={{0,1},{1,2},{2,3},{3,0},{4,5},{5,6},{6,7},{7,4},{8,9},{9,10},{10,1... | collective-permute-start | bytes 1966088 | tf_op jit(solution)/shard_map/ppermute | solution.py:39
  37.2 20.4 %collective-permute-start.8 = (bf16[640,512]{1,0:T(8,128)(2,1)S(1)}, bf16[640,512]{1,0:T(8,128)(2,1)S(1)}, u32[]{:S(2)}, u32[]{:S(2)}) collective-permute-start(bf16[640,512]{1,0:T(8,128)(2,1)S(1)} %get-tuple-element.37), channel_id=1, source_target_pairs={{0,3},{1,0},{2,1},{3,2},{4,7},{5,4},{6,5},{7,6},{8,11},{9,8},{10,9... | collective-permute-start | bytes 1966088 | tf_op jit(solution)/shard_map/ppermute | solution.py:39
  40.9 10.1 %collective-permute-start.15 = (bf16[160,512]{1,0:T(8,128)(2,1)S(1)}, bf16[160,512]{1,0:T(8,128)(2,1)S(1)}, u32[]{:S(2)}, u32[]{:S(2)}) collective-permute-start(bf16[160,512]{1,0:T(8,128)(2,1)S(1)} %add_convert_fusion.2), channel_id=1, source_target_pairs={{0,96},{1,97},{2,98},{3,99},{4,100},{5,101},{6,102},{7,103},{8,104... | collective-permute-start | bytes 491528 | tf_op jit(solution)/shard_map/ppermute | solution.py:39
  52.9 11.8 %collective-permute-start.16 = (bf16[160,512]{1,0:T(8,128)(2,1)S(1)}, bf16[160,512]{1,0:T(8,128)(2,1)S(1)}, u32[]{:S(2)}, u32[]{:S(2)}) collective-permute-start(bf16[160,512]{1,0:T(8,128)(2,1)S(1)} %add_convert_fusion.1), channel_id=1, source_target_pairs={{0,128},{1,129},{2,130},{3,131},{4,132},{5,133},{6,134},{7,135},{8... | collective-permute-start | bytes 491528 | tf_op jit(solution)/shard_map/ppermute | solution.py:39
  57.6 2.1 %copy-start.9 = (f32[640,512]{1,0:T(8,128)}, f32[640,512]{1,0:T(8,128)S(1)}, u32[]{:S(2)}) copy-start(f32[640,512]{1,0:T(8,128)S(1)} %get-tuple-element.40.own) | copy-start | bytes 3932164
  57.6 2.1 %copy-start.7 = (bf16[640,512]{1,0:T(8,128)(2,1)}, bf16[640,512]{1,0:T(8,128)(2,1)S(1)}, u32[]{:S(2)}) copy-start(bf16[640,512]{1,0:T(8,128)(2,1)S(1)} %collective-permute-done.7.left.refs_13_) | copy-start | bytes 1966084
  57.6 2.1 %copy-start.8 = (bf16[640,512]{1,0:T(8,128)(2,1)}, bf16[640,512]{1,0:T(8,128)(2,1)S(1)}, u32[]{:S(2)}) copy-start(bf16[640,512]{1,0:T(8,128)(2,1)S(1)} %collective-permute-done.8.right.refs_14_) | copy-start | bytes 1966084
  59.7 26.3 %collective-permute-start.9 = (bf16[640,512]{1,0:T(8,128)(2,1)}, bf16[640,512]{1,0:T(8,128)(2,1)}, u32[]{:S(2)}, u32[]{:S(2)}) collective-permute-start(bf16[640,512]{1,0:T(8,128)(2,1)} %get-tuple-element.38), channel_id=1, source_target_pairs={{0,4},{1,5},{2,6},{3,7},{4,0},{5,1},{6,2},{7,3},{8,12},{9,13},{10,... | collective-permute-start | bytes 1966088 | tf_op jit(solution)/shard_map/ppermute | solution.py:39
  62.0 24.1 %collective-permute-start.10 = (bf16[640,512]{1,0:T(8,128)(2,1)}, bf16[640,512]{1,0:T(8,128)(2,1)}, u32[]{:S(2)}, u32[]{:S(2)}) collective-permute-start(bf16[640,512]{1,0:T(8,128)(2,1)} %get-tuple-element.41), channel_id=1, source_target_pairs={{0,1},{1,2},{2,3},{3,0},{4,5},{5,6},{6,7},{7,4},{8,9},{9,10},{10,1... | collective-permute-start | bytes 1966088 | tf_op jit(solution)/shard_map/ppermute | solution.py:39
  63.2 22.8 %collective-permute-start.11 = (bf16[640,512]{1,0:T(8,128)(2,1)}, bf16[640,512]{1,0:T(8,128)(2,1)}, u32[]{:S(2)}, u32[]{:S(2)}) collective-permute-start(bf16[640,512]{1,0:T(8,128)(2,1)} %get-tuple-element.42), channel_id=1, source_target_pairs={{0,3},{1,0},{2,1},{3,2},{4,7},{5,4},{6,5},{7,6},{8,11},{9,8},{10,9... | collective-permute-start | bytes 1966088 | tf_op jit(solution)/shard_map/ppermute | solution.py:39
  64.7 4.8 %collective-permute-start.17 = (bf16[160,512]{1,0:T(8,128)(2,1)S(1)}, bf16[160,512]{1,0:T(8,128)(2,1)S(1)}, u32[]{:S(2)}, u32[]{:S(2)}) collective-permute-start(bf16[160,512]{1,0:T(8,128)(2,1)S(1)} %add_convert_fusion), channel_id=1, source_target_pairs={{0,16},{1,17},{2,18},{3,19},{4,20},{5,21},{6,22},{7,23},{8,24},{9,... | collective-permute-start | bytes 491528 | tf_op jit(solution)/shard_map/ppermute | solution.py:39
  70.4 12.5 %collective-permute-start.18 = (bf16[320,512]{1,0:T(8,128)(2,1)}, bf16[320,512]{1,0:T(8,128)(2,1)}, u32[]{:S(2)}, u32[]{:S(2)}) collective-permute-start(bf16[320,512]{1,0:T(8,128)(2,1)} %maximum_select_fusion.a), channel_id=1, source_target_pairs={{0,8},{1,9},{2,10},{3,11},{4,12},{5,13},{6,14},{7,15},{8,0},{9,1},... | collective-permute-start | bytes 983048 | tf_op jit(solution)/shard_map/ppermute | solution.py:39
  74.2 8.7 %copy-start.11 = (f32[640,512]{1,0:T(8,128)S(1)}, f32[640,512]{1,0:T(8,128)}, u32[]{:S(2)}) copy-start(f32[640,512]{1,0:T(8,128)} %mom.1) | copy-start | bytes 3932164
  74.2 8.7 %copy-start.12 = (f32[640,512]{1,0:T(8,128)S(1)}, f32[640,512]{1,0:T(8,128)}, u32[]{:S(2)}) copy-start(f32[640,512]{1,0:T(8,128)} %glob.1) | copy-start | bytes 3932164
  74.2 11.8 %copy-start.10 = (f32[640,512]{1,0:T(8,128)S(1)}, f32[640,512]{1,0:T(8,128)}, u32[]{:S(2)}) copy-start(f32[640,512]{1,0:T(8,128)} %copy-done.9) | copy-start | bytes 3932164
  82.9 3.1 %copy-start.2 = (bf16[256,5120]{1,0:T(8,128)(2,1)S(1)}, bf16[256,5120]{1,0:T(8,128)(2,1)}, u32[]{:S(2)}) copy-start(bf16[256,5120]{1,0:T(8,128)(2,1)} %xr.1) | copy-start | bytes 7864324
  82.9 3.1 %copy-start.5 = (bf16[256,512]{1,0:T(8,128)(2,1)S(1)}, bf16[256,512]{1,0:T(8,128)(2,1)}, u32[]{:S(2)}) copy-start(bf16[256,512]{1,0:T(8,128)(2,1)} %g.3) | copy-start | bytes 786436
  (3 other events, 2.9 us)
